TPU v7x, 128 devices: a whole 4x4x4 slice. The times are simulated.
128 devices in a mesh: sec: 8 (over z, core), dom: 16 (over y, x).
Axes of the slice: x: 4, y: 4, z: 4, core: 2. Of those that a mesh axis runs over, the one named last changes fastest.
Arguments:
- fluid_state: bfloat16 [5, 125, 262144], P(None, None, ('sec', 'dom')), may hold values from -6 to 6
- jac_inv: float32 [262144], P(('sec', 'dom')), may hold values from 0.5 to 2
- flux_mats: float32 [3, 5, 5], replicated, may hold values from -2 to 2
- neighbours: int32 [6, 262144], P(None, ('sec', 'dom')), may hold values from 0 to 2559
- surf_elem: int32 [65536], P(('sec', 'dom')), may hold values from 0 to 2047
- surf_node: int32 [65536], P(('sec', 'dom')), may hold values from 0 to 124
- normals: float32 [3, 65536], P(None, ('sec', 'dom')), may hold values from -6 to 6
- rbf_weights: float32 [16, 65536], P(None, ('sec', 'dom')), may hold values from 0 to 0.25
- owners: int32 [65536, 1], P(('sec', 'dom')), may hold values from 0 to 15; in each aligned block of 512 rows (0 to 511, 512 to 1023, ...) at most 128 rows name the same one
- patches: int32 [65536], P(('sec', 'dom')), may hold values from 0 to 255
- patch_nodes: int32 [16, 4096], P(None, 'dom'), may hold values from 0 to 1023
- shell_disp: float32 [3, 16384], P(None, 'dom'), may hold values from -6 to 6
- shell_vel: float32 [3, 16384], P(None, 'dom'), may hold values from -6 to 6
- mass_inv: float32 [16384], P('dom'), may hold values from 0.5 to 2
- shell_conn: int32 [4, 16384], P(None, 'dom'), may hold values from 0 to 1087
- elem_scale: float32 [16384], P('dom'), may hold values from 0.5 to 2
- elem_stiff: float32 [12, 12], replicated, may hold values from -1.75 to 1.75
Outputs:
- fluid_next: bfloat16 [5, 125, 262144], P(None, None, ('sec', 'dom'))
- shell_next: float32 [3, 16384], P(None, 'dom')
- face_shift: float32 [3, 65536], P(None, ('sec', 'dom'))
Inputs may be any that keep to these rules, and one draw needn't show every extreme that they name: `owners`: in the rows of one device no shell partition is named more than 128 times, a bound that some block reaches.
All inputs are finite; a program needn't handle non-finite values.
Results may differ from a plain program's by a relative error of at most 0.0065.
Values may be sent and summed in bfloat16 or wider, within the bound.
A program may use at most 128 MiB of HBM per device.

v0:
```python
import jax
import jax.numpy as jnp
import numpy as np
from jax import lax
from jax.sharding import PartitionSpec as P

STEPS = 2


LIFT = 10.0
FLOW_STEP = 0.02
SHELL_STEP = 0.3
HIGHEST = lax.Precision.HIGHEST


def extended(block, sides, width):
    for axis, dim in sides:
        count = lax.axis_size(axis)
        forward = [(i, i + 1) for i in range(count - 1)]
        backward = [(target, source) for source, target in forward]
        low = lax.ppermute(
            lax.slice_in_dim(block, block.shape[dim] - width, None, axis=dim), axis, forward
        )
        high = lax.ppermute(lax.slice_in_dim(block, 0, width, axis=dim), axis, backward)
        block = jnp.concatenate([low, block, high], axis=dim)
    return block


def lgl_derivative():
    points = np.array([-1.0, -np.sqrt(3.0 / 7.0), 0.0, np.sqrt(3.0 / 7.0), 1.0])
    barycentric = np.array(
        [
            1.0 / np.prod([points[col] - points[other] for other in range(5) if other != col])
            for col in range(5)
        ]
    )
    derivative = np.zeros((5, 5))
    for row in range(5):
        for col in range(5):
            if row != col:
                derivative[row, col] = (
                    barycentric[col] / barycentric[row] / (points[row] - points[col])
                )
        derivative[row, row] = -np.sum(derivative[row])
    return derivative.astype(np.float32)


def face_traces(cube):
    width = cube.shape[0]
    count = cube.shape[-1]
    faces = [
        cube[:, 0],
        cube[:, 4],
        cube[:, :, 0],
        cube[:, :, 4],
        cube[:, :, :, 0],
        cube[:, :, :, 4],
    ]
    return jnp.stack([face.reshape(width, 25, count) for face in faces])


def lift_faces(term_list, count):
    width = term_list.shape[1]
    shaped = term_list.reshape(6, width, 5, 5, count)
    lifted = jnp.zeros((width, 5, 5, 5, count), jnp.float32)
    lifted = lifted.at[:, 0].add(shaped[0])
    lifted = lifted.at[:, 4].add(shaped[1])
    lifted = lifted.at[:, :, 0].add(shaped[2])
    lifted = lifted.at[:, :, 4].add(shaped[3])
    lifted = lifted.at[:, :, :, 0].add(shaped[4])
    lifted = lifted.at[:, :, :, 4].add(shaped[5])
    return lifted


def fluid_tendency(cube, own_faces, extended_faces, neighbours, jac_inv, flux_mats):
    derivative = jnp.asarray(lgl_derivative())
    count = cube.shape[-1]
    width = cube.shape[0]
    extent = extended_faces.shape[-1]
    wide = cube.astype(jnp.float32)
    penalty = jnp.max(jnp.sum(jnp.abs(flux_mats), axis=2))
    flux_x = jnp.einsum("vw,wijke->vijke", flux_mats[0], wide, precision=HIGHEST)
    flux_y = jnp.einsum("vw,wijke->vijke", flux_mats[1], wide, precision=HIGHEST)
    flux_z = jnp.einsum("vw,wijke->vijke", flux_mats[2], wide, precision=HIGHEST)
    divergence = jnp.einsum("ai,vijke->vajke", derivative, flux_x, precision=HIGHEST)
    divergence = divergence + jnp.einsum("bj,vijke->vibke", derivative, flux_y, precision=HIGHEST)
    divergence = divergence + jnp.einsum("ck,vijke->vijce", derivative, flux_z, precision=HIGHEST)
    positions = jnp.arange(extent, dtype=jnp.int32)
    term_list = []
    for face in range(6):
        selector = (positions[:, None] == neighbours[face][None, :]).astype(jnp.bfloat16)
        source = extended_faces[face ^ 1].reshape(width * 25, extent)
        other = jnp.dot(source, selector, preferred_element_type=jnp.float32).reshape(
            width, 25, count
        )
        interface_jump = own_faces[face].astype(jnp.float32) - other
        sign = 1.0 if face % 2 else -1.0
        coupling_pass = 0.5 * (
            sign * flux_mats[face // 2] - penalty * jnp.eye(width, dtype=jnp.float32)
        )
        term_list.append(
            jnp.einsum("tk,kri->tri", coupling_pass, interface_jump, precision=HIGHEST)
        )
    lifted = lift_faces(jnp.stack(term_list), count)
    return jac_inv * (LIFT * lifted - divergence)


def patch_lookup(patch_nodes, row_patch):
    table_size = patch_nodes.shape[1]
    selector = (jnp.arange(table_size, dtype=jnp.int32)[:, None] == row_patch[None, :]).astype(
        jnp.float32
    )
    picked = jnp.dot(
        patch_nodes.astype(jnp.float32),
        selector,
        precision=HIGHEST,
        preferred_element_type=jnp.float32,
    )
    return picked.astype(jnp.int32)


def assemble(rows, row_patch, patch_nodes, size):
    node_list = patch_lookup(patch_nodes, row_patch[0])
    node_ids = jnp.arange(size, dtype=jnp.int32)

    def add_patch(forces, pair):
        nodes, weight = pair
        selector = (nodes[:, None] == node_ids[None, :]).astype(jnp.float32)
        return (
            forces
            + jnp.dot(
                rows[:3] * weight[None],
                selector,
                precision=HIGHEST,
                preferred_element_type=jnp.float32,
            ),
            None,
        )

    forces, unused = lax.scan(add_patch, jnp.zeros((3, size), jnp.float32), (node_list, rows[3:]))
    return forces


def on_device(
    fluid_state,
    jac_inv,
    flux_mats,
    neighbours,
    surf_elem,
    surf_node,
    normals,
    rbf_weights,
    owners,
    patches,
    patch_nodes,
    shell_disp,
    shell_vel,
    mass_inv,
    shell_conn,
    elem_scale,
    elem_stiff,
):
    width = fluid_state.shape[0]
    count = fluid_state.shape[2]
    halo_width = count // 8
    cube = fluid_state.reshape(width, 5, 5, 5, count)
    own_faces = face_traces(cube)
    extended_faces = extended(own_faces, ((("sec", "dom"), 3),), halo_width)
    tendency = fluid_tendency(cube, own_faces, extended_faces, neighbours, jac_inv, flux_mats)
    fluid_next = (
        fluid_state.astype(jnp.float32)
        + FLOW_STEP * tendency.reshape(width, fluid_state.shape[1], count)
    ).astype(jnp.bfloat16)
    elem_pick = (jnp.arange(count, dtype=jnp.int32)[:, None] == surf_elem[None, :]).astype(
        jnp.bfloat16
    )
    column_values = jnp.dot(fluid_next[4], elem_pick, preferred_element_type=jnp.float32)
    node_match = jnp.arange(fluid_state.shape[1], dtype=jnp.int32)[:, None] == surf_node[None, :]
    pressure = jnp.sum(jnp.where(node_match, column_values, 0.0), axis=0)
    traction = normals * pressure
    owner_dom = owners[:, 0]
    domains = lax.axis_size("dom")
    slot_limit = owners.shape[0] // 4
    one_hot = (owner_dom[:, None] == jnp.arange(domains, dtype=jnp.int32)[None, :]).astype(
        jnp.int32
    )
    ranks = jnp.cumsum(one_hot, axis=0) - 1
    slot_index = jnp.sum(ranks * one_hot, axis=1)
    target_slot = owner_dom * slot_limit + slot_index
    slot_match = target_slot[:, None] == jnp.arange(domains * slot_limit, dtype=jnp.int32)[None, :]
    placement_matrix = slot_match.astype(jnp.float32)
    payload = jnp.concatenate([traction, rbf_weights], axis=0)
    outgoing = jnp.dot(
        payload, placement_matrix, precision=HIGHEST, preferred_element_type=jnp.float32
    )
    outgoing_patch = jnp.sum(jnp.where(slot_match, patches[:, None], 0), axis=0)[None, :]
    incoming, incoming_patch = (
        lax.all_to_all(
            outgoing.astype(jnp.bfloat16), "dom", split_axis=1, concat_axis=1, tiled=True
        ).astype(outgoing.dtype),
        lax.all_to_all(outgoing_patch, "dom", split_axis=1, concat_axis=1, tiled=True),
    )
    nodes_here = shell_disp.shape[1]
    partial_force = assemble(incoming, incoming_patch, patch_nodes, nodes_here)
    external = lax.psum(partial_force, "sec")
    node_list = patch_lookup(patch_nodes, incoming_patch[0])
    rim = nodes_here // 32
    extent = nodes_here + 2 * rim
    extended_ids = jnp.arange(extent, dtype=jnp.int32)
    element_list = shell_conn.shape[1]
    displacement, velocity = (shell_disp, shell_vel)
    for substep in range(STEPS):
        extended_disp = extended(displacement, (("dom", 1),), rim)
        corner_values = []
        for corner in range(4):
            selector = (shell_conn[corner][:, None] == extended_ids[None, :]).astype(jnp.float32)
            corner_values.append(
                jnp.dot(
                    extended_disp, selector.T, precision=HIGHEST, preferred_element_type=jnp.float32
                )
            )
        picked = jnp.stack(corner_values, axis=1)
        elem_force = (
            jnp.dot(
                elem_stiff,
                picked.reshape(12, element_list),
                precision=HIGHEST,
                preferred_element_type=jnp.float32,
            )
            * elem_scale
        )
        shaped_force = elem_force.reshape(3, 4, element_list)
        internal = jnp.zeros((3, nodes_here), jnp.float32)
        for corner in range(4):
            selector = (
                shell_conn[corner][:, None] == extended_ids[None, rim : rim + nodes_here]
            ).astype(jnp.float32)
            internal = internal + jnp.dot(
                shaped_force[:, corner],
                selector,
                precision=HIGHEST,
                preferred_element_type=jnp.float32,
            )
        velocity = velocity + SHELL_STEP * mass_inv * (external - internal)
        displacement = displacement + SHELL_STEP * velocity
    node_ids = jnp.arange(nodes_here, dtype=jnp.int32)

    def read_patch(total, pair):
        nodes, weight = pair
        selector = (node_ids[:, None] == nodes[None, :]).astype(jnp.float32)
        values = jnp.dot(
            displacement, selector, precision=HIGHEST, preferred_element_type=jnp.float32
        )
        return (total + values * weight[None], None)

    shifted, unused = lax.scan(
        read_patch, jnp.zeros((3, incoming.shape[1]), jnp.float32), (node_list, incoming[3:])
    )
    returned = lax.all_to_all(shifted, "dom", split_axis=1, concat_axis=1, tiled=True)
    face_shift = jnp.dot(
        returned, placement_matrix.T, precision=HIGHEST, preferred_element_type=jnp.float32
    )
    return (fluid_next, displacement, face_shift)


def solution(mesh):
    return jax.shard_map(
        on_device,
        mesh=mesh,
        in_specs=(
            P(None, None, ("sec", "dom")),
            P(("sec", "dom")),
            P(),
            P(None, ("sec", "dom")),
            P(("sec", "dom")),
            P(("sec", "dom")),
            P(None, ("sec", "dom")),
            P(None, ("sec", "dom")),
            P(("sec", "dom"), None),
            P(("sec", "dom")),
            P(None, "dom"),
            P(None, "dom"),
            P(None, "dom"),
            P("dom"),
            P(None, "dom"),
            P("dom"),
            P(),
        ),
        out_specs=(P(None, None, ("sec", "dom")), P(None, "dom"), P(None, ("sec", "dom"))),
        check_vma=False,
    )
```

profile of v0, /device:TPU:0, one launch (start us, length us, event | category | flops | bytes accessed | tf_op | source)
XLA Modules:
  0.0 410.0 jit_solution(14072863242883093197)
XLA Ops:
  0.6 5.3 %reshape.411 = bf16[5,5,5,5,2048]{4,3,2,1,0:T(8,128)(2,1)} reshape(bf16[5,125,2048]{2,1,0:T(8,128)(2,1)} %param.34) | data formatting | bytes 5120000 | tf_op jit(solution)/shard_map/reshape | solution.py:166
  6.0 3.5 fusion.291
  38.2 4.4 %collective-permute-start = (bf16[6,5,25,256]{3,2,1,0:T(8,128)(2,1)}, bf16[6,5,25,256]{3,2,1,0:T(8,128)(2,1)}, u32[]{:S(2)}, u32[]{:S(2)}) collective-permute-start(bf16[6,5,25,256]{3,2,1,0:T(8,128)(2,1)} %get-tuple-element.211), channel_id=1, source_target_pairs={{0,1},{1,2},{2,3},{3,4},{4,5},{5,6},{6,7},{7,8},{8,9},{9,10},{10,1... | collective-permute-start | bytes 1152008 | tf_op jit(solution)/shard_map/ppermute | solution.py:21
  46.6 7.4 %all-to-all-start.1 = ((s32[1,16,128]{2,0,1:T(1,128)}), s32[1,16,128]{2,0,1:T(1,128)S(1)}, u32[]{:S(2)}, u32[]{:S(2)}) async-start(s32[1,16,128]{2,0,1:T(1,128)} %bitcast.76), calls=%async_computation.1 | async-start | bytes 16384 | tf_op jit(solution)/shard_map/all_to_all | solution.py:201
  54.1 3.8 collective-permute-start.2
  64.9 7.5 %fusion.76 = f32[5,5,5,5,2048]{4,0,3,2,1:T(8,128)S(1)} fusion(bf16[5,5,5,5,2048]{4,3,2,1,0:T(8,128)(2,1)} %reshape.411, f32[1,5,5]{2,0,1:T(1,128)S(1)} %get-tuple-element.237), kind=kOutput, calls=%fused_computation.91 | convolution fusion | flops 76800000 | bytes 7680100 | tf_op jit(solution)/shard_map/vw,wijke->vijke/dot_general | solution.py:84
  72.5 4.6 %fusion.78 = f32[5,5,5,5,2048]{4,0,3,2,1:T(8,128)S(1)} fusion(bf16[5,5,5,5,2048]{4,3,2,1,0:T(8,128)(2,1)S(1)} %copy-done.2, f32[1,5,5]{2,0,1:T(1,128)S(1)} %get-tuple-element.236), kind=kOutput, calls=%fused_computation.93 | convolution fusion | flops 76800000 | bytes 7680100 | tf_op jit(solution)/shard_map/vw,wijke->vijke/dot_general | solution.py:83
  77.1 18.9 %fusion.42 = f32[5,5,5,2048,5]{3,4,2,1,0:T(8,128)} fusion(f32[5,5,1,1,1]{1,0,4,3,2:T(8,128)S(1)} %copy-done.13, f32[5,5,5,5,2048]{4,0,3,2,1:T(8,128)S(1)} %fusion.76), kind=kOutput, calls=%fused_computation.48 | convolution fusion | flops 76800000 | bytes 10240100 | tf_op jit(solution)/shard_map/ck,vijke->vijce/dot_general | solution.py:87
  96.0 18.9 %fusion.44 = f32[5,5,5,2048,5]{3,4,2,1,0:T(8,128)} fusion(f32[5,5,1,1,1]{1,0,4,3,2:T(8,128)S(1)} %copy-done.13, f32[5,5,5,5,2048]{4,0,3,2,1:T(8,128)S(1)} %fusion.78), kind=kOutput, calls=%fused_computation.50 | convolution fusion | flops 76800000 | bytes 10240100 | tf_op jit(solution)/shard_map/bj,vijke->vibke/dot_general | solution.py:86
  115.0 4.6 %fusion.80 = f32[5,5,5,5,2048]{4,0,3,2,1:T(8,128)S(1)} fusion(bf16[5,5,5,5,2048]{4,3,2,1,0:T(8,128)(2,1)S(1)} %copy-done.2, f32[1,5,5]{2,0,1:T(1,128)S(1)} %get-tuple-element.235), kind=kOutput, calls=%fused_computation.95 | convolution fusion | flops 76800000 | bytes 7680100 | tf_op jit(solution)/shard_map/vw,wijke->vijke/dot_general | solution.py:82
  119.6 19.1 %fusion.46 = f32[5,5,5,2048,5]{3,4,2,1,0:T(8,128)} fusion(f32[5,5,1,1,1]{1,0,4,3,2:T(8,128)S(1)} %copy-done.13, f32[5,5,5,5,2048]{4,0,3,2,1:T(8,128)S(1)} %fusion.80), kind=kOutput, calls=%fused_computation.52 | convolution fusion | flops 76800000 | bytes 10240100 | tf_op jit(solution)/shard_map/ai,vijke->vajke/dot_general | solution.py:85
  157.1 3.5 pad_maximum_fusion
  160.6 4.5 %fusion.94 = f32[25,2048,5]{1,0,2:T(8,128)S(1)} fusion(f32[5,25,2048]{2,1,0:T(8,128)S(1)} %copy-done.8, s32[2048]{0:T(1024)S(1)} %bitcast.391, bf16[6,5,25,2560]{3,2,1,0:T(8,128)(2,1)S(1)} %pad_maximum_fusion), kind=kOutput, calls=%fused_computation.113 | convolution fusion | flops 1316218880 | bytes 3162112 | tf_op jit(solution)/shard_map/dot_general | solution.py:93
  165.8 4.5 %fusion.100 = f32[25,2048,5]{1,0,2:T(8,128)S(1)} fusion(f32[5,25,2048]{2,1,0:T(8,128)S(1)} %copy-done.10, s32[2048]{0:T(1024)S(1)} %bitcast.390, bf16[6,5,25,2560]{3,2,1,0:T(8,128)(2,1)S(1)} %pad_maximum_fusion), kind=kOutput, calls=%fused_computation.115 | convolution fusion | flops 1316218880 | bytes 3162112 | tf_op jit(solution)/shard_map/dot_general | solution.py:93
  170.9 4.9 %fusion.106 = f32[25,2048,5]{1,0,2:T(8,128)S(1)} fusion(f32[5,25,2048]{2,1,0:T(8,128)S(1)} %copy-done.9, s32[2048]{0:T(1024)S(1)} %bitcast.389, bf16[6,5,25,2560]{3,2,1,0:T(8,128)(2,1)S(1)} %pad_maximum_fusion), kind=kOutput, calls=%fused_computation.117 | convolution fusion | flops 1316218880 | bytes 3162112 | tf_op jit(solution)/shard_map/dot_general | solution.py:93
  176.5 4.5 %fusion.112 = f32[25,2048,5]{1,0,2:T(8,128)S(1)} fusion(f32[5,25,2048]{2,1,0:T(8,128)S(1)} %reshape.426, s32[2048]{0:T(1024)S(1)} %bitcast.388, bf16[6,5,25,2560]{3,2,1,0:T(8,128)(2,1)S(1)} %pad_maximum_fusion), kind=kOutput, calls=%fused_computation.119 | convolution fusion | flops 1316218880 | bytes 3162112 | tf_op jit(solution)/shard_map/dot_general | solution.py:93
  181.6 4.5 %fusion.118 = f32[25,2048,5]{1,0,2:T(8,128)S(1)} fusion(f32[5,25,2048]{2,1,0:T(8,128)S(1)} %copy-done.12, s32[2048]{0:T(1024)S(1)} %bitcast.387, bf16[6,5,25,2560]{3,2,1,0:T(8,128)(2,1)S(1)} %pad_maximum_fusion), kind=kOutput, calls=%fused_computation.121 | convolution fusion | flops 1316218880 | bytes 3162112 | tf_op jit(solution)/shard_map/dot_general | solution.py:93
  186.8 4.7 %fusion.124 = f32[25,2048,5]{1,0,2:T(8,128)S(1)} fusion(f32[5,25,2048]{2,1,0:T(8,128)S(1)} %copy-done.11, s32[2048]{0:T(1024)S(1)} %bitcast.386, bf16[6,5,25,2560]{3,2,1,0:T(8,128)(2,1)S(1)} %pad_maximum_fusion), kind=kOutput, calls=%fused_computation.123 | convolution fusion | flops 1316218880 | bytes 3162112 | tf_op jit(solution)/shard_map/dot_general | solution.py:93
  207.3 21.8 %fusion.41 = f32[5,5,5,5,2048]{4,0,3,2,1:T(8,128)} fusion(f32[5,5,5,2048,5]{3,4,2,1,0:T(8,128)} %fusion.42, f32[5,5,5,2048,5]{3,4,2,1,0:T(8,128)} %fusion.44, f32[5,5,5,2048,5]{3,4,2,1,0:T(8,128)} %fusion.46, f32[5,5,5,5,2048]{4,0,3,2,1:T(8,128)S(1)} %fusion.90, f32[2048]{0:T(1024)S(1)} %copy-done.21), kind=kLoop, calls=%fused_computation.46 | loop fusion | flops 7680000 | bytes 25608192 | tf_op jit(solution)/shard_map/mul | solution.py:172
  229.1 6.4 %fusion.64 = bf16[5,125,2048]{2,1,0:T(8,128)(2,1)S(1)} fusion(f32[5,125,2048]{2,0,1:T(8,128)} %bitcast.368, bf16[5,125,2048]{2,1,0:T(8,128)(2,1)S(1)} %copy-done.3), kind=kLoop, calls=%fused_computation.71 | loop fusion | flops 3840000 | bytes 10240000 | tf_op jit(solution)/shard_map/convert_element_type | solution.py:173
  238.7 7.9 %all-to-all-start = ((bf16[19,16,128]{2,0,1:T(8,128)(2,1)}), bf16[19,16,128]{2,0,1:T(8,128)(2,1)S(1)}, u32[]{:S(2)}, u32[]{:S(2)}) async-start(bf16[19,16,128]{2,0,1:T(8,128)(2,1)} %copy.148), calls=%async_computation | async-start | bytes 196608 | tf_op jit(solution)/shard_map/all_to_all | solution.py:198
  247.4 7.1 %all-to-all-done = bf16[19,16,128]{2,0,1:T(8,128)(2,1)S(1)} async-done(((bf16[19,16,128]{2,0,1:T(8,128)(2,1)}), bf16[19,16,128]{2,0,1:T(8,128)(2,1)S(1)}, u32[]{:S(2)}, u32[]{:S(2)}) %all-to-all-start) | async-done | bytes 77856 | tf_op jit(solution)/shard_map/all_to_all | solution.py:198
  254.6 44.8 %while.28 = (s32[]{:T(128)}, f32[3,1024]{1,0:T(4,128)S(1)}, f32[19,2048]{1,0:T(8,128)S(1)}, f32[16,2048]{1,0:T(8,128)S(1)}, s32[16,2048]{1,0:T(8,128)S(1)}, /*index=5*/s32[]{:T(128)}, s32[]{:T(128)}) while((s32[]{:T(128)}, f32[3,1024]{1,0:T(4,128)S(1)}, f32[19,2048]{1,0:T(8,128)S(1)}, f32[16,2048]{1,0:T(8,128)S(1)}, ...), condition=%wide.region_8.9_spmd.clone, body=%wide.region_7.0_spmd.clone.sunk | while | flops 77606912 | bytes 110687 | solution.py:140
  254.7 2.7 fusion.330
  257.5 2.7 fusion.330
  260.3 2.7 fusion.330
  263.1 2.7 fusion.330
  265.9 2.7 fusion.330
  299.4 25.0 %psum.7 = f32[3,1024]{1,0:T(4,128)S(1)} all-reduce(f32[3,1024]{1,0:T(4,128)S(1)} %get-tuple-element.139), channel_id=1, replica_groups=mesh['sec'=8,'dom'=16] {'sec'}, use_global_device_ids=true, to_apply=%region_9.10 | all-reduce | flops 3072 | bytes 24576 | tf_op jit(solution)/shard_map/psum | solution.py:205
  329.8 4.0 collective-permute-done.5
  348.6 43.6 %while.29 = (s32[]{:T(128)}, f32[3,2048]{1,0:T(4,128)S(1)}, s32[16,2048]{1,0:T(8,128)S(1)}, f32[3,1024]{1,0:T(4,128)S(1)}, f32[16,2048]{1,0:T(8,128)S(1)}, /*index=5*/s32[]{:T(128)}, s32[]{:T(128)}) while((s32[]{:T(128)}, f32[3,2048]{1,0:T(4,128)S(1)}, s32[16,2048]{1,0:T(8,128)S(1)}, f32[3,1024]{1,0:T(4,128)S(1)}, ...), condition=%wide.region_11.12_spmd.clone, body=%wide.region_10.11_spmd.clone.sunk | while | flops 77613056 | bytes 110687 | solution.py:256
  392.3 14.9 %all_to_all.30 = f32[3,16,128]{2,0,1:T(4,128)S(1)} all-to-all(f32[3,16,128]{2,0,1:T(4,128)S(1)} %bitcast.383), channel_id=1, replica_groups=mesh['sec'=8,'dom'=16] {'dom'}, dimensions={1} | all-to-all | bytes 49152 | tf_op jit(solution)/shard_map/all_to_all | solution.py:259
  (259 shorter events, 177.3 us)
Async XLA Ops:
  0.6 152.1 %copy-start = (f32[12,12]{1,0:T(8,128)S(1)}, f32[12,12]{1,0:T(8,128)}, u32[]{:S(2)}) copy-start(f32[12,12]{1,0:T(8,128)} %param.50) | copy-start | bytes 1732
  28.0 6.2 %copy-start.6 = (bf16[1,5,25,2048]{3,2,1,0:T(8,128)(2,1)S(1)}, bf16[1,5,25,2048]{3,2,1,0:T(8,128)(2,1)}, u32[]{:S(2)}) copy-start(bf16[1,5,25,2048]{3,2,1,0:T(8,128)(2,1)} %stack_reshape_squeeze.22) | copy-start | bytes 1536004
  28.0 7.1 %copy-start.7 = (bf16[1,5,25,2048]{3,2,1,0:T(8,128)(2,1)S(1)}, bf16[1,5,25,2048]{3,2,1,0:T(8,128)(2,1)}, u32[]{:S(2)}) copy-start(bf16[1,5,25,2048]{3,2,1,0:T(8,128)(2,1)} %stack_reshape_squeeze.23) | copy-start | bytes 1536004
  28.0 15.9 %copy-start.17 = (s32[512,1]{0,1:T(1,128)S(1)}, s32[512,1]{0,1:T(1,128)}, u32[]{:S(2)}) copy-start(s32[512,1]{0,1:T(1,128)} %param.42) | copy-start | bytes 6148
  28.0 17.4 %copy-start.23 = (s32[512]{0:T(512)S(1)}, s32[512]{0:T(512)}, u32[]{:S(2)}) copy-start(s32[512]{0:T(512)} %param.43) | copy-start | bytes 6148
  28.0 26.0 %copy-start.16 = (f32[3,1024]{1,0:T(4,128)S(1)}, f32[3,1024]{1,0:T(4,128)}, u32[]{:S(2)}) copy-start(f32[3,1024]{1,0:T(4,128)} %param.45) | copy-start | bytes 36868
  28.0 31.7 %copy-start.15 = (f32[3,5,5]{2,0,1:T(4,128)S(1)}, f32[3,5,5]{2,0,1:T(4,128)}, u32[]{:S(2)}) copy-start(f32[3,5,5]{2,0,1:T(4,128)} %param.36) | copy-start | bytes 904
  38.2 26.7 %copy-start.14 = (s32[6,2048]{1,0:T(8,128)S(1)}, s32[6,2048]{1,0:T(8,128)}, u32[]{:S(2)}) copy-start(s32[6,2048]{1,0:T(8,128)} %param.37) | copy-start | bytes 147460
  38.2 118.9 %collective-permute-start = (bf16[6,5,25,256]{3,2,1,0:T(8,128)(2,1)}, bf16[6,5,25,256]{3,2,1,0:T(8,128)(2,1)}, u32[]{:S(2)}, u32[]{:S(2)}) collective-permute-start(bf16[6,5,25,256]{3,2,1,0:T(8,128)(2,1)} %get-tuple-element.211), channel_id=1, source_target_pairs={{0,1},{1,2},{2,3},{3,4},{4,5},{5,6},{6,7},{7,8},{8,9},{9,10},{10,1... | collective-permute-start | bytes 1152008 | tf_op jit(solution)/shard_map/ppermute | solution.py:21
  42.6 114.5 %collective-permute-start.1 = (bf16[6,5,25,256]{3,2,1,0:T(8,128)(2,1)}, bf16[6,5,25,256]{3,2,1,0:T(8,128)(2,1)}, u32[]{:S(2)}, u32[]{:S(2)}) collective-permute-start(bf16[6,5,25,256]{3,2,1,0:T(8,128)(2,1)} %get-tuple-element.212), channel_id=1, source_target_pairs={{1,0},{2,1},{3,2},{4,3},{5,4},{6,5},{7,6},{8,7},{9,8},{10,9},{11,1... | collective-permute-start | bytes 1152008 | tf_op jit(solution)/shard_map/ppermute | solution.py:24
  46.6 192.1 %all-to-all-start.1 = ((s32[1,16,128]{2,0,1:T(1,128)}), s32[1,16,128]{2,0,1:T(1,128)S(1)}, u32[]{:S(2)}, u32[]{:S(2)}) async-start(s32[1,16,128]{2,0,1:T(1,128)} %bitcast.76), calls=%async_computation.1 | async-start | bytes 16384 | tf_op jit(solution)/shard_map/all_to_all | solution.py:201
  54.1 89.5 %collective-permute-start.2 = (f32[3,32]{1,0:T(4,128)S(1)}, f32[3,32]{1,0:T(4,128)S(1)}, u32[]{:S(2)}, u32[]{:S(2)}) collective-permute-start(f32[3,32]{1,0:T(4,128)S(1)} %get-tuple-element.234), channel_id=1, source_target_pairs={{0,1},{1,2},{2,3},{3,4},{4,5},{5,6},{6,7},{7,8},{8,9},{9,10},{10,1... | collective-permute-start | bytes 1160 | tf_op jit(solution)/shard_map/ppermute | solution.py:21
  57.9 85.6 %collective-permute-start.3 = (f32[3,32]{1,0:T(4,128)S(1)}, f32[3,32]{1,0:T(4,128)S(1)}, u32[]{:S(2)}, u32[]{:S(2)}) collective-permute-start(f32[3,32]{1,0:T(4,128)S(1)} %get-tuple-element.233), channel_id=1, source_target_pairs={{1,0},{2,1},{3,2},{4,3},{5,4},{6,5},{7,6},{8,7},{9,8},{10,9},{11,1... | collective-permute-start | bytes 1160 | tf_op jit(solution)/shard_map/ppermute | solution.py:24
  64.9 7.5 %copy-start.2 = (bf16[5,5,5,5,2048]{4,3,2,1,0:T(8,128)(2,1)S(1)}, bf16[5,5,5,5,2048]{4,3,2,1,0:T(8,128)(2,1)}, u32[]{:S(2)}) copy-start(bf16[5,5,5,5,2048]{4,3,2,1,0:T(8,128)(2,1)} %reshape.411) | copy-start | bytes 7680004
  119.6 19.2 %copy-start.19 = (s32[4,1024]{1,0:T(4,128)S(1)}, s32[4,1024]{1,0:T(4,128)}, u32[]{:S(2)}) copy-start(s32[4,1024]{1,0:T(4,128)} %param.48) | copy-start | bytes 49156
  119.6 19.2 %copy-start.22 = (f32[1024]{0:T(1024)S(1)}, f32[1024]{0:T(1024)}, u32[]{:S(2)}) copy-start(f32[1024]{0:T(1024)} %param.47) | copy-start | bytes 12292
  142.7 10.1 %copy-start.18 = (f32[1024]{0:T(1024)S(1)}, f32[1024]{0:T(1024)}, u32[]{:S(2)}) copy-start(f32[1024]{0:T(1024)} %param.49) | copy-start | bytes 12292
  160.6 5.2 %copy-start.10 = (f32[5,25,2048]{2,1,0:T(8,128)S(1)}, f32[5,25,2048]{2,1,0:T(8,128)}, u32[]{:S(2)}) copy-start(f32[5,25,2048]{2,1,0:T(8,128)} %reshape.424) | copy-start | bytes 3072004
  165.8 5.1 %copy-start.9 = (f32[5,25,2048]{2,1,0:T(8,128)S(1)}, f32[5,25,2048]{2,1,0:T(8,128)}, u32[]{:S(2)}) copy-start(f32[5,25,2048]{2,1,0:T(8,128)} %reshape.425) | copy-start | bytes 3072004
  176.5 5.1 %copy-start.12 = (f32[5,25,2048]{2,1,0:T(8,128)S(1)}, f32[5,25,2048]{2,1,0:T(8,128)}, u32[]{:S(2)}) copy-start(f32[5,25,2048]{2,1,0:T(8,128)} %reshape.427) | copy-start | bytes 3072004
  207.2 21.8 %copy-start.3 = (bf16[5,125,2048]{2,1,0:T(8,128)(2,1)S(1)}, bf16[5,125,2048]{2,1,0:T(8,128)(2,1)}, u32[]{:S(2)}) copy-start(bf16[5,125,2048]{2,1,0:T(8,128)(2,1)} %param.34) | copy-start | bytes 7680004
  229.1 6.5 %copy-start.27 = (s32[512]{0:T(512)S(1)}, s32[512]{0:T(512)}, u32[]{:S(2)}) copy-start(s32[512]{0:T(512)} %param.38) | copy-start | bytes 6148
  229.1 6.5 %copy-start.28 = (s32[512]{0:T(512)S(1)}, s32[512]{0:T(512)}, u32[]{:S(2)}) copy-start(s32[512]{0:T(512)} %param.39) | copy-start | bytes 6148
  229.1 7.3 %copy-start.20 = (f32[3,512]{1,0:T(4,128)S(1)}, f32[3,512]{1,0:T(4,128)}, u32[]{:S(2)}) copy-start(f32[3,512]{1,0:T(4,128)} %param.40) | copy-start | bytes 18436
  229.1 7.3 %copy-start.24 = (f32[16,512]{1,0:T(8,128)S(1)}, f32[16,512]{1,0:T(8,128)}, u32[]{:S(2)}) copy-start(f32[16,512]{1,0:T(8,128)} %param.41) | copy-start | bytes 98308
  235.6 19.0 %copy-start.5 = (bf16[5,125,2048]{2,1,0:T(8,128)(2,1)}, bf16[5,125,2048]{2,1,0:T(8,128)(2,1)S(1)}, u32[]{:S(2)}) copy-start(bf16[5,125,2048]{2,1,0:T(8,128)(2,1)S(1)} %fusion.64) | copy-start | bytes 7680004
  235.6 11.0 %copy-start.25 = (s32[16,256]{1,0:T(8,128)S(1)}, s32[16,256]{1,0:T(8,128)}, u32[]{:S(2)}) copy-start(s32[16,256]{1,0:T(8,128)} %param.44) | copy-start | bytes 49156
  238.7 15.8 %all-to-all-start = ((bf16[19,16,128]{2,0,1:T(8,128)(2,1)}), bf16[19,16,128]{2,0,1:T(8,128)(2,1)S(1)}, u32[]{:S(2)}, u32[]{:S(2)}) async-start(bf16[19,16,128]{2,0,1:T(8,128)(2,1)} %copy.148), calls=%async_computation | async-start | bytes 196608 | tf_op jit(solution)/shard_map/all_to_all | solution.py:198
  254.6 69.8 %copy-start.26 = (f32[3,1024]{1,0:T(4,128)S(1)}, f32[3,1024]{1,0:T(4,128)}, u32[]{:S(2)}) copy-start(f32[3,1024]{1,0:T(4,128)} %param.46) | copy-start | bytes 36868
  325.8 3.9 collective-permute-start.4
  328.3 5.5 %collective-permute-start.5 = (f32[3,32]{1,0:T(4,128)S(1)}, f32[3,32]{1,0:T(4,128)S(1)}, u32[]{:S(2)}, u32[]{:S(2)}) collective-permute-start(f32[3,32]{1,0:T(4,128)S(1)} %get-tuple-element.227), channel_id=1, source_target_pairs={{1,0},{2,1},{3,2},{4,3},{5,4},{6,5},{7,6},{8,7},{9,8},{10,9},{11,1... | collective-permute-start | bytes 1160 | tf_op jit(solution)/shard_map/ppermute | solution.py:24
  392.2 17.5 %copy-start.29 = (f32[3,1024]{1,0:T(4,128)}, f32[3,1024]{1,0:T(4,128)S(1)}, u32[]{:S(2)}) copy-start(f32[3,1024]{1,0:T(4,128)S(1)} %get-tuple-element.356) | copy-start | bytes 36868
  (6 other events, 26.0 us)
where the time goes:
time: 415 us; the launch traced here: 410 us
  matrix products  237 us (57%)
  local copies, waits for them, and re-layouts  48.4 us (12%)
  other arithmetic  40.8 us (10%)
  blocking collectives  39.9 us (10%)
  starting transfers between devices  30.6 us (7%)
  waiting for transfers between devices  11.1 us (3%)
    dot_general x16, matrix products, add_patch(): jnp.dot(rows[:3] * weight[None], selector, precision=HIGHEST, preferred_e...  44 us
    dot_general x16, matrix products, read_patch(): jnp.dot(displacement, selector, precision=HIGHEST, preferred_element_type...  42.5 us
    dot_general x6, matrix products, fluid_tendency(): jnp.dot(source, selector, preferred_element_type=jnp.float32)  27.5 us
    psum x1, blocking collectives, on_device(): external = lax.psum(partial_force, 'sec')  25 us
    mul x1, other arithmetic, on_device(): FLOW_STEP * tendency.reshape(width, fluid_state.shape[1], count)  21.8 us
    dot_general x1, matrix products, fluid_tendency(): jnp.einsum('ai,vijke->vajke', derivative, flux_x, precision=HIGHEST)  19.1 us
    dot_general x1, matrix products, fluid_tendency(): jnp.einsum('ck,vijke->vijce', derivative, flux_z, precision=HIGHEST)  18.9 us
    dot_general x1, matrix products, fluid_tendency(): jnp.einsum('bj,vijke->vibke', derivative, flux_y, precision=HIGHEST)  18.9 us
  transfers between devices with their start and end apart: 8, of which 2 were waited for; matrix products, arithmetic and copies ran while one was open for 44% of the time, Pallas kernels for 0%

commit v1 on v0

v1 whole, which is shorter than its diff:
```python
import jax
import jax.numpy as jnp
import numpy as np
from jax import lax
from jax.experimental import pallas as pl
from jax.experimental.pallas import tpu as pltpu
from jax.sharding import PartitionSpec as P

VARS, NP, K, STEPS = 5, 125, 16, 2
E, F, PATCHES, S, SE = 2048, 512, 256, 1024, 1024
HALO, HS, CAP = 256, 32, 128
N_SEC, N_DOM = 8, 16
LIFT, FLOW_STEP, SHELL_STEP = 10.0, 0.02, 0.3

TILE = 256
PART = 512
PARTS = (E + 2 * HALO) // PART
ROWS = VARS * 128
DEPTH = ROWS + 6 * 128
BF, F32, I32 = jnp.bfloat16, jnp.float32, jnp.int32
HIGHEST = lax.Precision.HIGHEST
MESH = pl.DeviceIdType.MESH


def lgl_derivative():
    points = np.array([-1.0, -np.sqrt(3.0 / 7.0), 0.0, np.sqrt(3.0 / 7.0), 1.0])
    barycentric = np.array(
        [
            1.0 / np.prod([points[col] - points[other] for other in range(5) if other != col])
            for col in range(5)
        ]
    )
    derivative = np.zeros((5, 5))
    for row in range(5):
        for col in range(5):
            if row != col:
                derivative[row, col] = (
                    barycentric[col] / barycentric[row] / (points[row] - points[col])
                )
        derivative[row, row] = -np.sum(derivative[row])
    return derivative.astype(np.float32)


def constants():
    nodes = np.arange(NP).reshape(5, 5, 5)
    faces = [nodes[0], nodes[4], nodes[:, 0], nodes[:, 4], nodes[:, :, 0], nodes[:, :, 4]]
    faces = [face.reshape(25) for face in faces]
    d, eye = lgl_derivative(), np.eye(5, dtype=np.float32)
    own = np.zeros((4, 128, 128), np.float32)
    own[0, :NP, :NP] = -np.kron(np.kron(d, eye), eye)
    own[1, :NP, :NP] = -np.kron(np.kron(eye, d), eye)
    own[2, :NP, :NP] = -np.kron(np.kron(eye, eye), d)
    for face in range(6):
        sign = 1.0 if face % 2 else -1.0
        for node in faces[face]:
            own[face // 2, node, node] += sign * 0.5 * LIFT
            own[3, node, node] -= 0.5 * LIFT
    select = np.zeros((VARS, 6 * 32, 128), np.float32)
    place = np.zeros((6, 128, 128), np.float32)
    for face in range(6):
        for n in range(25):
            for w in range(VARS):
                select[w, face * 32 + w + n, faces[face ^ 1][n]] = 1.0
                place[face, faces[face][n], 25 * w + n] = -0.5 * LIFT
    return own, select.astype(jnp.bfloat16), place.astype(jnp.bfloat16)


def dot(a, b):
    return jnp.dot(a, b, preferred_element_type=F32)


def dot_t(a, b):
    return lax.dot_general(a, b, (((1,), (1,)), ((), ())), preferred_element_type=F32)


def halves(x):
    high = x.astype(BF)
    low = (x - high.astype(F32)).astype(BF)
    return jnp.concatenate([high, low], axis=0)


def joined(y):
    rows = y.shape[0] // 2
    return y[:rows] + y[rows:]


def iota(shape, dim):
    return lax.broadcasted_iota(I32, shape, dim)


def one_hot(ids, rows):
    return (iota((rows, ids.shape[1]), 0) == ids).astype(F32)


def kernel(
    u_ref, jac_ref, flux_ref, nb_ref, selem_ref, snode_ref, normal_ref, weight_ref, owner_ref,
    patch_ref, pnode_ref, disp_ref, vel_ref, minv_ref, conn_ref, scale_ref, stiff_ref,
    own_ref, select_ref, place_ref,
    fluid_ref, shell_ref, shift_ref,
    x_ref, src_ref, ab_ref, hlo_ref, hhi_ref, o4_ref,
    ohp_ref, ohn_ref, maskn_ref, ohc_ref, maskc_ref, mask8_ref, ohs_ref,
    wsend_ref, wrecv_ref, wall_ref, tsend_ref, trecv_ref, rsend_ref, rrecv_ref,
    ebuf_ref, erecv_ref, edge_ref, rim_ref, d_ref, v_ref, m_ref,
    flow_s, flow_r, w_s, w_r, t_s, t_r, r_s, r_r, e_s, e_r, rim_s, rim_r,
):
    sec, dom = lax.axis_index("sec"), lax.axis_index("dom")
    line = sec * N_DOM + dom
    devices = N_SEC * N_DOM
    nxt, prv = lax.rem(line + 1, devices), lax.rem(line + devices - 1, devices)
    right = (nxt // N_DOM, lax.rem(nxt, N_DOM))
    left = (prv // N_DOM, lax.rem(prv, N_DOM))

    def dom_peer(d):
        return (sec, lax.rem(dom + d, N_DOM))

    def sec_peer(d):
        return (lax.rem(sec + d, N_SEC), dom)

    def copy(src, dst, send, recv, device):
        return pltpu.make_async_remote_copy(
            src_ref=src, dst_ref=dst, send_sem=send, recv_sem=recv, device_id=device, device_id_type=MESH
        )

    barrier = pltpu.get_barrier_semaphore()
    greeted = [dom_peer(d) for d in range(1, N_DOM)] + [sec_peer(d) for d in range(1, N_SEC)] + [right, left]
    for device in greeted:
        pl.semaphore_signal(barrier, inc=1, device_id=device, device_id_type=MESH)

    for v in range(VARS):
        x_ref[v * 128 + 112 : v * 128 + 128, :] = jnp.zeros((16, E), BF)
        x_ref[v * 128 : v * 128 + NP, :] = u_ref[v]

    for h in range(8):
        lanes = slice(h * 128, (h + 1) * 128)
        m_ref[h : h + 1, :] = minv_ref[:, lanes]
        for c in range(3):
            d_ref[c * 8 + h : c * 8 + h + 1, :] = disp_ref[c : c + 1, lanes]
            v_ref[c * 8 + h : c * 8 + h + 1, :] = vel_ref[c : c + 1, lanes]

    relative = (owner_ref[...] - dom + N_DOM) & (N_DOM - 1)
    owned = one_hot(relative, N_DOM)
    earlier = (iota((F, F), 0) < iota((F, F), 1)).astype(F32).astype(BF)
    rank = jnp.sum(owned * dot(owned.astype(BF), earlier), axis=0, keepdims=True).astype(I32)
    ohs_ref[...] = one_hot(rank, CAP).astype(BF)

    payload = jnp.concatenate([weight_ref[...], patch_ref[...].astype(F32), jnp.zeros((15, F), F32)], axis=0)
    payload = jnp.concatenate([payload * owned[d : d + 1] for d in range(N_DOM)], axis=0)
    placed = dot_t(payload.astype(BF), ohs_ref[...])
    wsend_ref[...] = placed.astype(BF).reshape(N_DOM, 32, CAP)

    def edges(step):
        for c in range(3):
            edge_ref[step, 0, c : c + 1, :] = d_ref[c * 8 : c * 8 + 1, :]
            edge_ref[step, 1, c : c + 1, :] = d_ref[c * 8 + 7 : c * 8 + 8, :]

    def rims(step):
        return [
            copy(edge_ref.at[step, 0], rim_ref.at[step, 0], rim_s.at[step, 0], rim_r.at[step, 0], dom_peer(N_DOM - 1)),
            copy(edge_ref.at[step, 1], rim_ref.at[step, 1], rim_s.at[step, 1], rim_r.at[step, 1], dom_peer(1)),
        ]

    edge_ref[...] = jnp.zeros(edge_ref.shape, F32)
    edges(0)

    pl.semaphore_wait(barrier, len(greeted))
    flow = [
        copy(x_ref.at[0:ROWS, E - HALO : E], hlo_ref, flow_s.at[0], flow_r.at[0], right),
        copy(x_ref.at[0:ROWS, 0:HALO], hhi_ref, flow_s.at[1], flow_r.at[1], left),
    ]
    for c in flow:
        c.start()
    early = [copy(wsend_ref.at[d], wrecv_ref.at[d], w_s.at[d], w_r.at[d], dom_peer(d)) for d in range(1, N_DOM)]
    for c in early:
        c.start()
    wrecv_ref[0] = wsend_ref[0]
    rim0 = rims(0)
    for c in rim0:
        c.start()

    penalty = None
    for d in range(3):
        for v in range(VARS):
            total = jnp.abs(flux_ref[d, v, 0])
            for w in range(1, VARS):
                total = total + jnp.abs(flux_ref[d, v, w])
            penalty = total if penalty is None else jnp.maximum(penalty, total)
    for v in range(VARS):
        for w in range(VARS):
            block = flux_ref[0, v, w] * own_ref[0] + flux_ref[1, v, w] * own_ref[1] + flux_ref[2, v, w] * own_ref[2]
            if v == w:
                block = block + penalty * own_ref[3]
            ab_ref[v * 128 : v * 128 + 128, w * 128 : w * 128 + 128] = block.astype(BF)
    column = iota((1, 128), 1)
    for face in range(6):
        sign = 1.0 if face % 2 else -1.0
        where = place_ref[face].astype(F32)
        for v in range(VARS):
            factor = jnp.zeros((1, 128), F32)
            for w in range(VARS):
                value = sign * flux_ref[face // 2, v, w]
                if v == w:
                    value = value - penalty
                factor = jnp.where((column >= 25 * w) & (column < 25 * w + 25), value, factor)
            ab_ref[v * 128 : v * 128 + 128, ROWS + face * 128 : ROWS + face * 128 + 128] = (where * factor).astype(BF)

    def extract(values, part, lanes):
        e = [dot(select_ref[w], values(w)) for w in range(VARS)]
        for face in range(6):
            g = [x[face * 32 : face * 32 + 32] for x in e]
            pieces = [g[0][0:24]]
            for w in range(1, VARS):
                pieces += [g[w - 1][24:32] + g[w][0:8], g[w][8:24]]
            pieces += [g[VARS - 1][24:32]]
            src_ref[face, pl.ds(part * 128, 128), lanes] = jnp.concatenate(pieces, axis=0).astype(BF)

    for part in range(E // PART):
        for half in range(PART // TILE):
            cols = slice(part * PART + half * TILE, part * PART + (half + 1) * TILE)
            extract(lambda w: x_ref[w * 128 : w * 128 + 128, cols], part, slice(half * TILE, (half + 1) * TILE))

    for k in range(K):
        ids = pnode_ref[k : k + 1, :]
        lanes = slice(k * PATCHES, (k + 1) * PATCHES)
        ohn_ref[:, lanes] = one_hot(ids & 127, 128).astype(BF)
        maskn_ref[:, lanes] = one_hot(ids >> 7, 8)
    for q in range(4):
        ids = conn_ref[q : q + 1, :]
        ids = jnp.where(ids >= HS, ids - HS, ids + (S + 128 - HS))
        lanes = slice(q * SE, (q + 1) * SE)
        ohc_ref[:, lanes] = one_hot(ids & 127, 128).astype(BF)
        maskc_ref[:, lanes] = one_hot(ids >> 7, 8)
        mask8_ref[:, lanes] = ((ids >> 7) == 8).astype(F32)

    for c in flow:
        c.wait()
    keep_hi = jnp.where(line < devices - 1, 1.0, 0.0).astype(BF)
    keep_lo = jnp.where(line > 0, 1.0, 0.0).astype(BF)
    extract(lambda w: hhi_ref[w * 128 : w * 128 + 128, :] * keep_hi, PARTS - 1, slice(0, HALO))
    extract(lambda w: hlo_ref[w * 128 : w * 128 + 128, :] * keep_lo, PARTS - 1, slice(HALO, 2 * HALO))

    def gather(t, carry):
        cols = pl.ds(pl.multiple_of(t * TILE, TILE), TILE)
        for face in range(6):
            ids = nb_ref[face : face + 1, cols]
            ids = jnp.where(ids >= HALO, ids - HALO, ids + (E + HALO))
            picked = dot(src_ref[face], one_hot(ids & (PART - 1), PART).astype(BF))
            part = ids // PART
            other = picked[0:128]
            for p in range(1, PARTS):
                other = jnp.where(part == p, picked[p * 128 : p * 128 + 128], other)
            x_ref[ROWS + face * 128 : ROWS + face * 128 + 128, cols] = other.astype(BF)
        factor = FLOW_STEP * jac_ref[:, cols]
        v = VARS - 1
        moved = x_ref[v * 128 : v * 128 + 128, cols].astype(F32) + factor * dot(
            ab_ref[v * 128 : v * 128 + 128, :], x_ref[:, cols]
        )
        moved = moved.astype(BF)
        o4_ref[:, cols] = moved
        fluid_ref[v, :, cols] = moved[:NP]
        return carry

    lax.fori_loop(0, E // TILE, gather, 0)

    elems = selem_ref[...]
    picker = one_hot(elems & (TILE - 1), TILE).astype(BF)
    found = jnp.zeros((128, F), F32)
    for h in range(E // TILE):
        found = jnp.where((elems // TILE) == h, dot(o4_ref[:, h * TILE : (h + 1) * TILE], picker), found)
    pressure = jnp.sum(jnp.where(iota((128, F), 0) == snode_ref[...], found, 0.0), axis=0, keepdims=True)
    traction = jnp.concatenate([normal_ref[...] * pressure, jnp.zeros((5, F), F32)], axis=0)
    rows = jnp.concatenate([traction * owned[d : d + 1] for d in range(N_DOM)], axis=0)
    tsend_ref[...] = joined(dot_t(halves(rows), ohs_ref[...])).reshape(N_DOM, 8, CAP)
    loads = [copy(tsend_ref.at[d], trecv_ref.at[d], t_s.at[d], t_r.at[d], dom_peer(d)) for d in range(1, N_DOM)]
    for c in loads:
        c.start()
    trecv_ref[0] = tsend_ref[0]

    def advance(t, carry):
        cols = pl.ds(pl.multiple_of(t * TILE, TILE), TILE)
        factor = FLOW_STEP * jac_ref[:, cols]
        change = dot(ab_ref[0 : 4 * 128, :], x_ref[:, cols])
        for v in range(VARS - 1):
            moved = x_ref[v * 128 : v * 128 + 128, cols].astype(F32) + factor * change[v * 128 : v * 128 + 128]
            fluid_ref[v, :, cols] = moved.astype(BF)[:NP]
        return carry

    lax.fori_loop(0, E // TILE, advance, 0)

    for c in early:
        c.wait()
    for d in range(N_DOM):
        block = wrecv_ref[d].astype(F32)
        wall_ref[:, d * CAP : (d + 1) * CAP] = block[0:K]
        ohp_ref[:, d * CAP : (d + 1) * CAP] = one_hot(block[K : K + 1].astype(I32), PATCHES).astype(BF)

    def internal(step):
        lane = iota((8, 128), 1)
        from_right = rim_ref[step, 0] * jnp.where(dom < N_DOM - 1, 1.0, 0.0)
        from_left = rim_ref[step, 1] * jnp.where(dom > 0, 1.0, 0.0)
        rim = jnp.where(lane < 64, from_right, from_left)
        read = joined(dot(halves(jnp.concatenate([d_ref[...], rim], axis=0)), ohc_ref[...]))
        picked = []
        for c in range(3):
            values = jnp.sum(read[c * 8 : c * 8 + 8] * maskc_ref[...], axis=0, keepdims=True)
            values = values + read[24 + c : 25 + c] * mask8_ref[...]
            picked += [values[:, q * SE : (q + 1) * SE] for q in range(4)]
        force = jnp.dot(
            stiff_ref[...], jnp.concatenate(picked, axis=0), precision=HIGHEST, preferred_element_type=F32
        )
        force = force * scale_ref[...]
        spread = []
        for c in range(3):
            line_c = jnp.concatenate([force[c * 4 + q : c * 4 + q + 1] for q in range(4)], axis=1)
            spread.append(line_c * maskc_ref[...])
        return joined(dot_t(halves(jnp.concatenate(spread, axis=0)), ohc_ref[...]))

    for c in rim0:
        c.wait()
    inner = internal(0)

    for c in loads:
        c.wait()
    load = []
    for c in range(3):
        line_c = jnp.concatenate([trecv_ref[d, c : c + 1, :] for d in range(N_DOM)], axis=1)
        load.append(wall_ref[...] * line_c)
    by_patch = joined(dot_t(halves(jnp.concatenate(load, axis=0)), ohp_ref[...]))
    spread = []
    for c in range(3):
        line_c = jnp.concatenate([by_patch[c * K + k : c * K + k + 1] for k in range(K)], axis=1)
        spread.append(line_c * maskn_ref[...])
    partial = joined(dot_t(halves(jnp.concatenate(spread, axis=0)), ohn_ref[...]))
    ebuf_ref[...] = partial
    sums = [copy(ebuf_ref, erecv_ref.at[d], e_s.at[d], e_r.at[d], sec_peer(d)) for d in range(1, N_SEC)]
    for c in sums:
        c.start()
    erecv_ref[0] = partial
    for c in sums:
        c.wait()
    external = erecv_ref[lax.rem(sec, N_SEC)]
    for s in range(1, N_SEC):
        external = external + erecv_ref[lax.rem(sec - s + N_SEC, N_SEC)]

    mass = jnp.concatenate([m_ref[...]] * 3, axis=0)
    for step in range(STEPS):
        if step > 0:
            edges(step)
            around = rims(step)
            for c in around:
                c.start()
            for c in around:
                c.wait()
            inner = internal(step)
        velocity = v_ref[...] + SHELL_STEP * mass * (external - inner)
        v_ref[...] = velocity
        d_ref[...] = d_ref[...] + SHELL_STEP * velocity

    read = joined(dot(halves(d_ref[...]), ohn_ref[...]))
    nodes = []
    for c in range(3):
        values = jnp.sum(read[c * 8 : c * 8 + 8] * maskn_ref[...], axis=0, keepdims=True)
        nodes += [values[:, k * PATCHES : (k + 1) * PATCHES] for k in range(K)]
    by_row = joined(dot(halves(jnp.concatenate(nodes, axis=0)), ohp_ref[...]))
    rsend_ref[...] = jnp.zeros(rsend_ref.shape, F32)
    for c in range(3):
        total = jnp.sum(by_row[c * K : (c + 1) * K] * wall_ref[...], axis=0, keepdims=True)
        for d in range(N_DOM):
            rsend_ref[d, c : c + 1, :] = total[:, d * CAP : (d + 1) * CAP]
    returns = [
        copy(rsend_ref.at[d], rrecv_ref.at[d], r_s.at[d], r_r.at[d], dom_peer(N_DOM - d)) for d in range(1, N_DOM)
    ]
    for c in returns:
        c.start()
    rrecv_ref[0] = rsend_ref[0]
    for h in range(8):
        for c in range(3):
            shell_ref[c : c + 1, h * 128 : (h + 1) * 128] = d_ref[c * 8 + h : c * 8 + h + 1, :]
    for c in returns:
        c.wait()
    back = joined(dot(halves(rrecv_ref[...].reshape(N_DOM * 8, CAP)), ohs_ref[...]))
    shift = back[0:8] * owned[0:1]
    for d in range(1, N_DOM):
        shift = shift + back[d * 8 : d * 8 + 8] * owned[d : d + 1]
    shift_ref[...] = shift[0:3]


def on_device(
    fluid_state, jac_inv, flux_mats, neighbours, surf_elem, surf_node, normals, rbf_weights, owners,
    patches, patch_nodes, shell_disp, shell_vel, mass_inv, shell_conn, elem_scale, elem_stiff,
):
    own, select, place = constants()
    vmem, smem = pl.BlockSpec(memory_space=pltpu.VMEM), pl.BlockSpec(memory_space=pltpu.SMEM)
    dma = pltpu.SemaphoreType.DMA
    return pl.pallas_call(
        kernel,
        out_shape=(
            jax.ShapeDtypeStruct((VARS, NP, E), BF),
            jax.ShapeDtypeStruct((3, S), F32),
            jax.ShapeDtypeStruct((3, F), F32),
        ),
        in_specs=[vmem, vmem, smem] + [vmem] * 17,
        out_specs=(vmem, vmem, vmem),
        scratch_shapes=[
            pltpu.VMEM((DEPTH, E), BF),
            pltpu.VMEM((6, PARTS * 128, PART), BF),
            pltpu.VMEM((ROWS, DEPTH), BF),
            pltpu.VMEM((ROWS, HALO), BF),
            pltpu.VMEM((ROWS, HALO), BF),
            pltpu.VMEM((128, E), BF),
            pltpu.VMEM((PATCHES, N_DOM * CAP), BF),
            pltpu.VMEM((128, K * PATCHES), BF),
            pltpu.VMEM((8, K * PATCHES), F32),
            pltpu.VMEM((128, 4 * SE), BF),
            pltpu.VMEM((8, 4 * SE), F32),
            pltpu.VMEM((1, 4 * SE), F32),
            pltpu.VMEM((CAP, F), BF),
            pltpu.VMEM((N_DOM, 32, CAP), BF),
            pltpu.VMEM((N_DOM, 32, CAP), BF),
            pltpu.VMEM((K, N_DOM * CAP), F32),
            pltpu.VMEM((N_DOM, 8, CAP), F32),
            pltpu.VMEM((N_DOM, 8, CAP), F32),
            pltpu.VMEM((N_DOM, 8, CAP), F32),
            pltpu.VMEM((N_DOM, 8, CAP), F32),
            pltpu.VMEM((24, 128), F32),
            pltpu.VMEM((N_SEC, 24, 128), F32),
            pltpu.VMEM((STEPS, 2, 8, 128), F32),
            pltpu.VMEM((STEPS, 2, 8, 128), F32),
            pltpu.VMEM((24, 128), F32),
            pltpu.VMEM((24, 128), F32),
            pltpu.VMEM((8, 128), F32),
            dma((2,)), dma((2,)),
            dma((N_DOM,)), dma((N_DOM,)),
            dma((N_DOM,)), dma((N_DOM,)),
            dma((N_DOM,)), dma((N_DOM,)),
            dma((N_SEC,)), dma((N_SEC,)),
            dma((STEPS, 2)), dma((STEPS, 2)),
        ],
        compiler_params=pltpu.CompilerParams(
            collective_id=0, has_side_effects=True, vmem_limit_bytes=56 * 1024 * 1024
        ),
    )(
        fluid_state, jac_inv.reshape(1, E), flux_mats, neighbours, surf_elem.reshape(1, F),
        surf_node.reshape(1, F), normals, rbf_weights, owners.reshape(1, F), patches.reshape(1, F),
        patch_nodes, shell_disp, shell_vel, mass_inv.reshape(1, S), shell_conn,
        elem_scale.reshape(1, SE), elem_stiff, jnp.asarray(own), jnp.asarray(select), jnp.asarray(place),
    )


def solution(mesh):
    flow, shell = ("sec", "dom"), "dom"
    return jax.shard_map(
        on_device,
        mesh=mesh,
        in_specs=(
            P(None, None, flow),
            P(flow),
            P(),
            P(None, flow),
            P(flow),
            P(flow),
            P(None, flow),
            P(None, flow),
            P(flow, None),
            P(flow),
            P(None, shell),
            P(None, shell),
            P(None, shell),
            P(shell),
            P(None, shell),
            P(shell),
            P(),
        ),
        out_specs=(P(None, None, flow), P(None, shell), P(None, flow)),
        check_vma=False,
    )
```

time: 415 us -> 65.2 us (0.16); the launches traced: 410 us -> 65 us
  matrix products: 237 us -> 0 us
  Pallas kernels: 0 us -> 58.3 us
  local copies, waits for them, and re-layouts: 48.4 us -> 6.09 us
  other arithmetic: 40.8 us -> 0 us
  blocking collectives: 39.9 us -> 0 us
  starting transfers between devices: 30.6 us -> 0 us
  waiting for transfers between devices: 11.1 us -> 0 us
    dot_general x72 -> x0, matrix products: 237 us -> none  [the longest x16 44 us: add_patch(): jnp.dot(rows[:3] * weight[None], selector, precision=HIGHEST, preferred_e...]
    pallas_call x0 -> x1, Pallas kernels: none -> 58.3 us  [on_device(): pl.pallas_call(kernel, out_shape=(jax.ShapeDtypeStruct((VARS, NP, E), BF)...]
    psum x1 -> x0, blocking collectives: 25 us -> none  [on_device(): external = lax.psum(partial_force, 'sec')]
    mul x3 -> x0, other arithmetic: 21.8 us -> none  [the longest x1 21.8 us: on_device(): FLOW_STEP * tendency.reshape(width, fluid_state.shape[1], count)]
    all_to_all x2 -> x0, starting transfers between devices: 15.4 us -> none  [the longest x1 7.94 us: on_device(): lax.all_to_all(outgoing.astype(jnp.bfloat16), 'dom', split_axis=1, concat...]
    ppermute x6 -> x0, starting transfers between devices: 15.2 us -> none  [the longest x3 10.7 us: extended(): lax.ppermute(lax.slice_in_dim(block, block.shape[dim] - width, None, axis...]
    all_to_all x1 -> x0, blocking collectives: 14.9 us -> none  [on_device(): lax.all_to_all(shifted, 'dom', split_axis=1, concat_axis=1, tiled=True)]
    another operation x17 -> x0, local copies, waits for them, and re-layouts: 13.6 us -> none  [the longest x7 9.51 us: face_traces(): return jnp.stack([face.reshape(width, 25, count) for face in faces])]
  transfers between devices with their start and end apart: 8 -> 0, of which waited for: 2 -> 0; matrix products, arithmetic and copies ran while one was open for 44% -> 0% of each run, Pallas kernels for 0% -> 0%
where the time goes in v1:
time: 65.2 us; the launch traced here: 65 us
  Pallas kernels  58.3 us (89%)
  local copies, waits for them, and re-layouts  6.09 us (9%)
  between operations  0.66 us (1%)
    pallas_call x1, Pallas kernels, on_device(): pl.pallas_call(kernel, out_shape=(jax.ShapeDtypeStruct((VARS, NP, E), BF)...  58.3 us
    unnamed x8, local copies, waits for them, and re-layouts  6.09 us

profile of v1, /device:TPU:0, one launch (start us, length us, event | category | flops | bytes accessed | tf_op | source)
XLA Modules:
  0.0 65.0 jit_solution(14741153175596764519)
XLA Ops:
  0.6 1.3 %copy.23.flux_ref = f32[3,5,5]{2,1,0:T(8,128)} copy(f32[3,5,5]{2,0,1:T(4,128)} %param.22) | data formatting | bytes 600 | tf_op args[2]
  1.9 58.3 %shard_map.211 = (bf16[5,125,2048]{2,1,0:T(8,128)(2,1)}, f32[3,1024]{1,0:T(4,128)}, f32[3,512]{1,0:T(4,128)}) custom-call(bf16[5,125,2048]{2,1,0:T(8,128)(2,1)} %u_ref.1, f32[1,2048]{1,0:T(1,128)} %bitcast.7, f32[3,5,5]{2,1,0:T(8,128)} %copy.23.flux_ref, s32[6,2048]{1,0:T(8,128)} %nb_ref.1, s32[1,512]{1,0:T(1,128)} %bitcast.10, s32[1,512]{1,0:T(1,128)} %bitcast.11, ...), custom_call_target="tpu_custom_call" | custom-call | tf_op jit(solution)/shard_map/pallas_call | solution.py:394
  60.2 0.0 copy-start
  60.2 0.0 copy-start.1
  60.2 3.6 %copy.27 = bf16[5,125,2048]{2,1,0:T(8,128)(2,1)} copy(bf16[5,125,2048]{2,1,0:T(8,128)(2,1)} %get-tuple-element.6) | data formatting | bytes 5120000
  63.8 0.0 copy-done
  63.8 0.6 copy.28
  64.4 0.0 copy-done.1
  64.4 0.6 copy.29
Async XLA Ops:
  60.2 3.6 %copy-start = (f32[3,1024]{1,0:T(4,128)S(1)}, f32[3,1024]{1,0:T(4,128)}, u32[]{:S(2)}) copy-start(f32[3,1024]{1,0:T(4,128)} %get-tuple-element.7) | copy-start | bytes 36868
  60.2 4.2 %copy-start.1 = (f32[3,512]{1,0:T(4,128)S(1)}, f32[3,512]{1,0:T(4,128)}, u32[]{:S(2)}) copy-start(f32[3,512]{1,0:T(4,128)} %get-tuple-element.8) | copy-start | bytes 18436

commit v2 on v1

--- a/solution.py
+++ b/solution.py
@@ -93,15 +93,15 @@
 
 
 def kernel(
-    u_ref, jac_ref, flux_ref, nb_ref, selem_ref, snode_ref, normal_ref, weight_ref, owner_ref,
+    state_ref, jac_ref, flux_ref, nb_ref, selem_ref, snode_ref, normal_ref, weight_ref, owner_ref,
     patch_ref, pnode_ref, disp_ref, vel_ref, minv_ref, conn_ref, scale_ref, stiff_ref,
-    own_ref, select_ref, place_ref,
+    own_hbm, select_hbm, place_hbm,
     fluid_ref, shell_ref, shift_ref,
-    x_ref, src_ref, ab_ref, hlo_ref, hhi_ref, o4_ref,
-    ohp_ref, ohn_ref, maskn_ref, ohc_ref, maskc_ref, mask8_ref, ohs_ref,
+    u_ref, own_ref, select_ref, place_ref, x_ref, src_ref, ab_ref, hlo_ref, hhi_ref,
+    surf_ref, ohp_ref, ohn_ref, maskn_ref, ohc_ref, maskc_ref, mask8_ref, ohs_ref,
     wsend_ref, wrecv_ref, wall_ref, tsend_ref, trecv_ref, rsend_ref, rrecv_ref,
     ebuf_ref, erecv_ref, edge_ref, rim_ref, d_ref, v_ref, m_ref,
-    flow_s, flow_r, w_s, w_r, t_s, t_r, r_s, r_r, e_s, e_r, rim_s, rim_r,
+    local_s, flow_s, flow_r, w_s, w_r, t_s, t_r, r_s, r_r, e_s, e_r, rim_s, rim_r,
 ):
     sec, dom = lax.axis_index("sec"), lax.axis_index("dom")
     line = sec * N_DOM + dom
@@ -126,9 +126,14 @@
     for device in greeted:
         pl.semaphore_signal(barrier, inc=1, device_id=device, device_id_type=MESH)
 
-    for v in range(VARS):
-        x_ref[v * 128 + 112 : v * 128 + 128, :] = jnp.zeros((16, E), BF)
-        x_ref[v * 128 : v * 128 + NP, :] = u_ref[v]
+    fetch = [
+        pltpu.make_async_copy(src, dst, local_s.at[i])
+        for i, (src, dst) in enumerate(
+            ((state_ref, u_ref), (own_hbm, own_ref), (select_hbm, select_ref), (place_hbm, place_ref))
+        )
+    ]
+    for c in fetch:
+        c.start()
 
     for h in range(8):
         lanes = slice(h * 128, (h + 1) * 128)
@@ -137,17 +142,6 @@
             d_ref[c * 8 + h : c * 8 + h + 1, :] = disp_ref[c : c + 1, lanes]
             v_ref[c * 8 + h : c * 8 + h + 1, :] = vel_ref[c : c + 1, lanes]
 
-    relative = (owner_ref[...] - dom + N_DOM) & (N_DOM - 1)
-    owned = one_hot(relative, N_DOM)
-    earlier = (iota((F, F), 0) < iota((F, F), 1)).astype(F32).astype(BF)
-    rank = jnp.sum(owned * dot(owned.astype(BF), earlier), axis=0, keepdims=True).astype(I32)
-    ohs_ref[...] = one_hot(rank, CAP).astype(BF)
-
-    payload = jnp.concatenate([weight_ref[...], patch_ref[...].astype(F32), jnp.zeros((15, F), F32)], axis=0)
-    payload = jnp.concatenate([payload * owned[d : d + 1] for d in range(N_DOM)], axis=0)
-    placed = dot_t(payload.astype(BF), ohs_ref[...])
-    wsend_ref[...] = placed.astype(BF).reshape(N_DOM, 32, CAP)
-
     def edges(step):
         for c in range(3):
             edge_ref[step, 0, c : c + 1, :] = d_ref[c * 8 : c * 8 + 1, :]
@@ -162,31 +156,35 @@
     edge_ref[...] = jnp.zeros(edge_ref.shape, F32)
     edges(0)
 
+    fetch[0].wait()
+    for v in range(VARS):
+        x_ref[v * 128 + 112 : v * 128 + 128, :] = jnp.zeros((16, E), BF)
+        x_ref[v * 128 : v * 128 + NP, :] = u_ref[v]
+
     pl.semaphore_wait(barrier, len(greeted))
+    rim0 = rims(0)
+    for c in rim0:
+        c.start()
     flow = [
         copy(x_ref.at[0:ROWS, E - HALO : E], hlo_ref, flow_s.at[0], flow_r.at[0], right),
         copy(x_ref.at[0:ROWS, 0:HALO], hhi_ref, flow_s.at[1], flow_r.at[1], left),
     ]
     for c in flow:
         c.start()
-    early = [copy(wsend_ref.at[d], wrecv_ref.at[d], w_s.at[d], w_r.at[d], dom_peer(d)) for d in range(1, N_DOM)]
-    for c in early:
-        c.start()
-    wrecv_ref[0] = wsend_ref[0]
-    rim0 = rims(0)
-    for c in rim0:
-        c.start()
-
+
+    for c in fetch[1:]:
+        c.wait()
     penalty = None
-    for d in range(3):
-        for v in range(VARS):
-            total = jnp.abs(flux_ref[d, v, 0])
-            for w in range(1, VARS):
-                total = total + jnp.abs(flux_ref[d, v, w])
-            penalty = total if penalty is None else jnp.maximum(penalty, total)
+    for v in range(VARS):
+        total = jnp.max(jnp.sum(jnp.abs(flux_ref[v]), axis=1, keepdims=True), axis=0, keepdims=True)
+        penalty = total if penalty is None else jnp.maximum(penalty, total)
+
+    def flux(d, v, w):
+        return flux_ref[v, d : d + 1, w : w + 1]
+
     for v in range(VARS):
         for w in range(VARS):
-            block = flux_ref[0, v, w] * own_ref[0] + flux_ref[1, v, w] * own_ref[1] + flux_ref[2, v, w] * own_ref[2]
+            block = flux(0, v, w) * own_ref[0] + flux(1, v, w) * own_ref[1] + flux(2, v, w) * own_ref[2]
             if v == w:
                 block = block + penalty * own_ref[3]
             ab_ref[v * 128 : v * 128 + 128, w * 128 : w * 128 + 128] = block.astype(BF)
@@ -197,7 +195,7 @@
         for v in range(VARS):
             factor = jnp.zeros((1, 128), F32)
             for w in range(VARS):
-                value = sign * flux_ref[face // 2, v, w]
+                value = sign * flux(face // 2, v, w)
                 if v == w:
                     value = value - penalty
                 factor = jnp.where((column >= 25 * w) & (column < 25 * w + 25), value, factor)
@@ -217,6 +215,37 @@
         for half in range(PART // TILE):
             cols = slice(part * PART + half * TILE, part * PART + (half + 1) * TILE)
             extract(lambda w: x_ref[w * 128 : w * 128 + 128, cols], part, slice(half * TILE, (half + 1) * TILE))
+
+    relative = (owner_ref[...] - dom + N_DOM) & (N_DOM - 1)
+    owned = one_hot(relative, N_DOM)
+    earlier = (iota((F, F), 0) < iota((F, F), 1)).astype(F32).astype(BF)
+    rank = jnp.sum(owned * dot(owned.astype(BF), earlier), axis=0, keepdims=True).astype(I32)
+    ohs_ref[...] = one_hot(rank, CAP).astype(BF)
+
+    payload = jnp.concatenate([weight_ref[...], patch_ref[...].astype(F32), jnp.zeros((15, F), F32)], axis=0)
+    payload = jnp.concatenate([payload * owned[d : d + 1] for d in range(N_DOM)], axis=0)
+    placed = dot_t(payload.astype(BF), ohs_ref[...])
+    wsend_ref[...] = placed.astype(BF).reshape(N_DOM, 32, CAP)
+
+    last = slice((VARS - 1) * 128, VARS * 128)
+    elems = selem_ref[...]
+    picker = one_hot(elems & (TILE - 1), TILE).astype(BF)
+    base, near = jnp.zeros((128, F), F32), jnp.zeros((16, F), F32)
+    for h in range(E // TILE):
+        cols = slice(h * TILE, (h + 1) * TILE)
+        factor = FLOW_STEP * jac_ref[:, cols]
+        moved = x_ref[last, cols].astype(F32) + factor * dot(ab_ref[last, 0:ROWS], x_ref[0:ROWS, cols])
+        ids = nb_ref[:, cols]
+        rows = jnp.concatenate(
+            [halves(factor), (ids & 255).astype(F32).astype(BF), (ids >> 8).astype(F32).astype(BF)], axis=0
+        )
+        rows = jnp.concatenate([halves(moved), rows, jnp.zeros((2, TILE), BF)], axis=0)
+        found = dot(rows, picker)
+        mine = (elems // TILE) == h
+        base = jnp.where(mine, joined(found[0:256]), base)
+        near = jnp.where(mine, found[256:272], near)
+    surf_factor = near[0:1] + near[1:2]
+    surf_near = near[2:8].astype(I32) + 256 * near[8:14].astype(I32)
 
     for k in range(K):
         ids = pnode_ref[k : k + 1, :]
@@ -230,68 +259,6 @@
         ohc_ref[:, lanes] = one_hot(ids & 127, 128).astype(BF)
         maskc_ref[:, lanes] = one_hot(ids >> 7, 8)
         mask8_ref[:, lanes] = ((ids >> 7) == 8).astype(F32)
-
-    for c in flow:
-        c.wait()
-    keep_hi = jnp.where(line < devices - 1, 1.0, 0.0).astype(BF)
-    keep_lo = jnp.where(line > 0, 1.0, 0.0).astype(BF)
-    extract(lambda w: hhi_ref[w * 128 : w * 128 + 128, :] * keep_hi, PARTS - 1, slice(0, HALO))
-    extract(lambda w: hlo_ref[w * 128 : w * 128 + 128, :] * keep_lo, PARTS - 1, slice(HALO, 2 * HALO))
-
-    def gather(t, carry):
-        cols = pl.ds(pl.multiple_of(t * TILE, TILE), TILE)
-        for face in range(6):
-            ids = nb_ref[face : face + 1, cols]
-            ids = jnp.where(ids >= HALO, ids - HALO, ids + (E + HALO))
-            picked = dot(src_ref[face], one_hot(ids & (PART - 1), PART).astype(BF))
-            part = ids // PART
-            other = picked[0:128]
-            for p in range(1, PARTS):
-                other = jnp.where(part == p, picked[p * 128 : p * 128 + 128], other)
-            x_ref[ROWS + face * 128 : ROWS + face * 128 + 128, cols] = other.astype(BF)
-        factor = FLOW_STEP * jac_ref[:, cols]
-        v = VARS - 1
-        moved = x_ref[v * 128 : v * 128 + 128, cols].astype(F32) + factor * dot(
-            ab_ref[v * 128 : v * 128 + 128, :], x_ref[:, cols]
-        )
-        moved = moved.astype(BF)
-        o4_ref[:, cols] = moved
-        fluid_ref[v, :, cols] = moved[:NP]
-        return carry
-
-    lax.fori_loop(0, E // TILE, gather, 0)
-
-    elems = selem_ref[...]
-    picker = one_hot(elems & (TILE - 1), TILE).astype(BF)
-    found = jnp.zeros((128, F), F32)
-    for h in range(E // TILE):
-        found = jnp.where((elems // TILE) == h, dot(o4_ref[:, h * TILE : (h + 1) * TILE], picker), found)
-    pressure = jnp.sum(jnp.where(iota((128, F), 0) == snode_ref[...], found, 0.0), axis=0, keepdims=True)
-    traction = jnp.concatenate([normal_ref[...] * pressure, jnp.zeros((5, F), F32)], axis=0)
-    rows = jnp.concatenate([traction * owned[d : d + 1] for d in range(N_DOM)], axis=0)
-    tsend_ref[...] = joined(dot_t(halves(rows), ohs_ref[...])).reshape(N_DOM, 8, CAP)
-    loads = [copy(tsend_ref.at[d], trecv_ref.at[d], t_s.at[d], t_r.at[d], dom_peer(d)) for d in range(1, N_DOM)]
-    for c in loads:
-        c.start()
-    trecv_ref[0] = tsend_ref[0]
-
-    def advance(t, carry):
-        cols = pl.ds(pl.multiple_of(t * TILE, TILE), TILE)
-        factor = FLOW_STEP * jac_ref[:, cols]
-        change = dot(ab_ref[0 : 4 * 128, :], x_ref[:, cols])
-        for v in range(VARS - 1):
-            moved = x_ref[v * 128 : v * 128 + 128, cols].astype(F32) + factor * change[v * 128 : v * 128 + 128]
-            fluid_ref[v, :, cols] = moved.astype(BF)[:NP]
-        return carry
-
-    lax.fori_loop(0, E // TILE, advance, 0)
-
-    for c in early:
-        c.wait()
-    for d in range(N_DOM):
-        block = wrecv_ref[d].astype(F32)
-        wall_ref[:, d * CAP : (d + 1) * CAP] = block[0:K]
-        ohp_ref[:, d * CAP : (d + 1) * CAP] = one_hot(block[K : K + 1].astype(I32), PATCHES).astype(BF)
 
     def internal(step):
         lane = iota((8, 128), 1)
@@ -318,6 +285,65 @@
         c.wait()
     inner = internal(0)
 
+    for c in flow:
+        c.wait()
+    early = [copy(wsend_ref.at[d], wrecv_ref.at[d], w_s.at[d], w_r.at[d], dom_peer(d)) for d in range(1, N_DOM)]
+    for c in early:
+        c.start()
+    wrecv_ref[0] = wsend_ref[0]
+    keep_hi = jnp.where(line < devices - 1, 1.0, 0.0).astype(BF)
+    keep_lo = jnp.where(line > 0, 1.0, 0.0).astype(BF)
+    extract(lambda w: hhi_ref[w * 128 : w * 128 + 128, :] * keep_hi, PARTS - 1, slice(0, HALO))
+    extract(lambda w: hlo_ref[w * 128 : w * 128 + 128, :] * keep_lo, PARTS - 1, slice(HALO, 2 * HALO))
+
+    def neighbour(face, ids):
+        ids = jnp.where(ids >= HALO, ids - HALO, ids + (E + HALO))
+        picked = dot(src_ref[face], one_hot(ids & (PART - 1), PART).astype(BF))
+        part = ids // PART
+        other = picked[0:128]
+        for p in range(1, PARTS):
+            other = jnp.where(part == p, picked[p * 128 : p * 128 + 128], other)
+        return other.astype(BF)
+
+    for half in range(F // TILE):
+        cols = slice(half * TILE, (half + 1) * TILE)
+        for face in range(6):
+            surf_ref[face * 128 : face * 128 + 128, cols] = neighbour(face, surf_near[face : face + 1, cols])
+    found = base + surf_factor * dot(ab_ref[last, ROWS:DEPTH], surf_ref[...])
+    found = found.astype(BF).astype(F32)
+    pressure = jnp.sum(jnp.where(iota((128, F), 0) == snode_ref[...], found, 0.0), axis=0, keepdims=True)
+    traction = jnp.concatenate([normal_ref[...] * pressure, jnp.zeros((5, F), F32)], axis=0)
+    rows = jnp.concatenate([traction * owned[d : d + 1] for d in range(N_DOM)], axis=0)
+    tsend_ref[...] = joined(dot_t(halves(rows), ohs_ref[...])).reshape(N_DOM, 8, CAP)
+    loads = [copy(tsend_ref.at[d], trecv_ref.at[d], t_s.at[d], t_r.at[d], dom_peer(d)) for d in range(1, N_DOM)]
+    for c in loads:
+        c.start()
+    trecv_ref[0] = tsend_ref[0]
+
+    def advance(t, carry):
+        cols = pl.ds(pl.multiple_of(t * TILE, TILE), TILE)
+        for face in range(6):
+            x_ref[ROWS + face * 128 : ROWS + face * 128 + 128, cols] = neighbour(face, nb_ref[face : face + 1, cols])
+        factor = FLOW_STEP * jac_ref[:, cols]
+        change = dot(ab_ref[...], x_ref[:, cols])
+        for v in range(VARS):
+            moved = x_ref[v * 128 : v * 128 + 128, cols].astype(F32) + factor * change[v * 128 : v * 128 + 128]
+            fluid_ref[v, :, cols] = moved.astype(BF)[:NP]
+        return carry
+
+    tiles = (2, 2, 2, 2)
+
+    def fill(wait):
+        lax.fori_loop(sum(tiles[:wait]), sum(tiles[: wait + 1]), advance, 0)
+
+    for c in early:
+        c.wait()
+    for d in range(N_DOM):
+        block = wrecv_ref[d].astype(F32)
+        wall_ref[:, d * CAP : (d + 1) * CAP] = block[0:K]
+        ohp_ref[:, d * CAP : (d + 1) * CAP] = one_hot(block[K : K + 1].astype(I32), PATCHES).astype(BF)
+    fill(0)
+
     for c in loads:
         c.wait()
     load = []
@@ -335,6 +361,7 @@
     for c in sums:
         c.start()
     erecv_ref[0] = partial
+    fill(1)
     for c in sums:
         c.wait()
     external = erecv_ref[lax.rem(sec, N_SEC)]
@@ -348,6 +375,7 @@
             around = rims(step)
             for c in around:
                 c.start()
+            fill(2)
             for c in around:
                 c.wait()
             inner = internal(step)
@@ -375,6 +403,7 @@
     for h in range(8):
         for c in range(3):
             shell_ref[c : c + 1, h * 128 : (h + 1) * 128] = d_ref[c * 8 + h : c * 8 + h + 1, :]
+    fill(3)
     for c in returns:
         c.wait()
     back = joined(dot(halves(rrecv_ref[...].reshape(N_DOM * 8, CAP)), ohs_ref[...]))
@@ -389,24 +418,28 @@
     patches, patch_nodes, shell_disp, shell_vel, mass_inv, shell_conn, elem_scale, elem_stiff,
 ):
     own, select, place = constants()
-    vmem, smem = pl.BlockSpec(memory_space=pltpu.VMEM), pl.BlockSpec(memory_space=pltpu.SMEM)
+    vmem, hbm = pl.BlockSpec(memory_space=pltpu.VMEM), pl.BlockSpec(memory_space=pl.ANY)
     dma = pltpu.SemaphoreType.DMA
     return pl.pallas_call(
         kernel,
         out_shape=(
-            jax.ShapeDtypeStruct((VARS, NP, E), BF),
-            jax.ShapeDtypeStruct((3, S), F32),
-            jax.ShapeDtypeStruct((3, F), F32),
+            pltpu.VMEM((VARS, NP, E), BF),
+            pltpu.VMEM((3, S), F32),
+            pltpu.VMEM((3, F), F32),
         ),
-        in_specs=[vmem, vmem, smem] + [vmem] * 17,
+        in_specs=[hbm] + [vmem] * 16 + [hbm] * 3,
         out_specs=(vmem, vmem, vmem),
         scratch_shapes=[
+            pltpu.VMEM((VARS, NP, E), BF),
+            pltpu.VMEM((4, 128, 128), F32),
+            pltpu.VMEM((VARS, 6 * 32, 128), BF),
+            pltpu.VMEM((6, 128, 128), BF),
             pltpu.VMEM((DEPTH, E), BF),
             pltpu.VMEM((6, PARTS * 128, PART), BF),
             pltpu.VMEM((ROWS, DEPTH), BF),
             pltpu.VMEM((ROWS, HALO), BF),
             pltpu.VMEM((ROWS, HALO), BF),
-            pltpu.VMEM((128, E), BF),
+            pltpu.VMEM((6 * 128, F), BF),
             pltpu.VMEM((PATCHES, N_DOM * CAP), BF),
             pltpu.VMEM((128, K * PATCHES), BF),
             pltpu.VMEM((8, K * PATCHES), F32),
@@ -428,7 +461,7 @@
             pltpu.VMEM((24, 128), F32),
             pltpu.VMEM((24, 128), F32),
             pltpu.VMEM((8, 128), F32),
-            dma((2,)), dma((2,)),
+            dma((4,)), dma((2,)), dma((2,)),
             dma((N_DOM,)), dma((N_DOM,)),
             dma((N_DOM,)), dma((N_DOM,)),
             dma((N_DOM,)), dma((N_DOM,)),
@@ -439,7 +472,7 @@
             collective_id=0, has_side_effects=True, vmem_limit_bytes=56 * 1024 * 1024
         ),
     )(
-        fluid_state, jac_inv.reshape(1, E), flux_mats, neighbours, surf_elem.reshape(1, F),
+        fluid_state, jac_inv.reshape(1, E), jnp.transpose(flux_mats, (1, 0, 2)), neighbours, surf_elem.reshape(1, F),
         surf_node.reshape(1, F), normals, rbf_weights, owners.reshape(1, F), patches.reshape(1, F),
         patch_nodes, shell_disp, shell_vel, mass_inv.reshape(1, S), shell_conn,
         elem_scale.reshape(1, SE), elem_stiff, jnp.asarray(own), jnp.asarray(select), jnp.asarray(place),

time: 65.2 us -> 49.5 us (0.76)
  Pallas kernels: 58.3 us -> 46 us
  local copies, waits for them, and re-layouts: 6.09 us -> 2.7 us
    pallas_call x1, Pallas kernels: 58.3 us -> 46 us  [on_device(): pl.pallas_call(kernel, out_shape=(pltpu.VMEM((VARS, NP, E), BF), pltpu.VM...]
    unnamed x8 -> x3, local copies, waits for them, and re-layouts: 6.09 us -> 2.7 us
where the time goes in v2:
time: 49.5 us; the launch traced here: 49.3 us
  Pallas kernels  46 us (93%)
  local copies, waits for them, and re-layouts  2.7 us (5%)
  between operations  0.65 us (1%)
    pallas_call x1, Pallas kernels, on_device(): pl.pallas_call(kernel, out_shape=(pltpu.VMEM((VARS, NP, E), BF), pltpu.VM...  46 us
    unnamed x3, local copies, waits for them, and re-layouts  2.7 us

profile of v2, /device:TPU:0, one launch (start us, length us, event | category | flops | bytes accessed | tf_op | source)
XLA Modules:
  0.0 49.3 jit_solution(6307683940368697838)
XLA Ops:
  0.6 46.0 %shard_map.211 = (bf16[5,125,2048]{2,1,0:T(8,128)(2,1)S(1)}, f32[3,1024]{1,0:T(4,128)S(1)}, f32[3,512]{1,0:T(4,128)S(1)}) custom-call(bf16[5,125,2048]{2,1,0:T(8,128)(2,1)} %state_ref.1, f32[1,2048]{1,0:T(1,128)} %bitcast.9, f32[5,3,5]{2,1,0:T(4,128)} %bitcast.8, s32[6,2048]{1,0:T(8,128)} %nb_ref.1, s32[1,512]{1,0:T(1,128)} %bitcast.12, s32[1,512]{1,0:T(1,128)} %bitcast.13, ...), custom_call_target="tpu_custom_call" | custom-call | tf_op jit(solution)/shard_map/pallas_call | solution.py:423
  46.6 1.5 %copy.26 = bf16[5,125,2048]{2,1,0:T(8,128)(2,1)} copy(bf16[5,125,2048]{2,1,0:T(8,128)(2,1)S(1)} %get-tuple-element.3) | data formatting | bytes 5120000
  48.1 0.6 %copy.28 = f32[3,512]{1,0:T(4,128)} copy(f32[3,512]{1,0:T(4,128)S(1)} %get-tuple-element.5) | data formatting | bytes 12288
  48.7 0.6 %copy.27 = f32[3,1024]{1,0:T(4,128)} copy(f32[3,1024]{1,0:T(4,128)S(1)} %get-tuple-element.4) | data formatting | bytes 24576

commit v3 on v2

--- a/solution.py
+++ b/solution.py
@@ -10,7 +10,7 @@
 E, F, PATCHES, S, SE = 2048, 512, 256, 1024, 1024
 HALO, HS, CAP = 256, 32, 128
 N_SEC, N_DOM = 8, 16
-LIFT, FLOW_STEP, SHELL_STEP = 10.0, 0.02, 0.3
+LIFT, _STEP, SHELL_STEP = 10.0, 0.02, 0.3
 
 TILE = 256
 PART = 512
@@ -98,10 +98,10 @@
     own_hbm, select_hbm, place_hbm,
     fluid_ref, shell_ref, shift_ref,
     u_ref, own_ref, select_ref, place_ref, x_ref, src_ref, ab_ref, hlo_ref, hhi_ref,
-    surf_ref, ohp_ref, ohn_ref, maskn_ref, ohc_ref, maskc_ref, mask8_ref, ohs_ref,
+    g_ref, gsend_ref, grecv_ref, ohp_ref, ohn_ref, maskn_ref, ohc_ref, maskc_ref, mask8_ref, ohs_ref,
     wsend_ref, wrecv_ref, wall_ref, tsend_ref, trecv_ref, rsend_ref, rrecv_ref,
     ebuf_ref, erecv_ref, edge_ref, rim_ref, d_ref, v_ref, m_ref,
-    local_s, flow_s, flow_r, w_s, w_r, t_s, t_r, r_s, r_r, e_s, e_r, rim_s, rim_r,
+    local_s, g_s, g_r, flow_s, flow_r, w_s, w_r, t_s, t_r, r_s, r_r, e_s, e_r, rim_s, rim_r,
 ):
     sec, dom = lax.axis_index("sec"), lax.axis_index("dom")
     line = sec * N_DOM + dom
@@ -121,6 +121,9 @@
             src_ref=src, dst_ref=dst, send_sem=send, recv_sem=recv, device_id=device, device_id_type=MESH
         )
 
+    def all_of(src, dst, send, recv):
+        return copy(src.at[1 : src.shape[0]], dst.at[1 : dst.shape[0]], send.at[0], recv.at[0], dom_peer(1))
+
     barrier = pltpu.get_barrier_semaphore()
     greeted = [dom_peer(d) for d in range(1, N_DOM)] + [sec_peer(d) for d in range(1, N_SEC)] + [right, left]
     for device in greeted:
@@ -156,12 +159,48 @@
     edge_ref[...] = jnp.zeros(edge_ref.shape, F32)
     edges(0)
 
+    relative = (owner_ref[...] - dom + N_DOM) & (N_DOM - 1)
+    owned = one_hot(relative, N_DOM)
+    earlier = (iota((F, F), 0) < iota((F, F), 1)).astype(F32).astype(BF)
+    rank = jnp.sum(owned * dot(owned.astype(BF), earlier), axis=0, keepdims=True).astype(I32)
+    ohs_ref[...] = one_hot(rank, CAP).astype(BF)
+
+    penalty = None
+    for v in range(VARS):
+        total = jnp.max(jnp.sum(jnp.abs(flux_ref[v]), axis=1, keepdims=True), axis=0, keepdims=True)
+        penalty = total if penalty is None else jnp.maximum(penalty, total)
+
+    def flux(d, v, w):
+        return flux_ref[v, d : d + 1, w : w + 1]
+
+
+    def coupling(face, v, w):
+        value = (1.0 if face % 2 else -1.0) * flux(face // 2, v, w)
+        return value - penalty if v == w else value
+
     fetch[0].wait()
     for v in range(VARS):
         x_ref[v * 128 + 112 : v * 128 + 128, :] = jnp.zeros((16, E), BF)
         x_ref[v * 128 : v * 128 + NP, :] = u_ref[v]
 
+    for c in fetch[1:]:
+        c.wait()
+    choice = select_ref[0].astype(F32) * (-0.5 * LIFT)
+    couple = []
+    for w in range(VARS):
+        blocks = [choice[face * 32 : face * 32 + 32] * coupling(face, VARS - 1, w) for face in range(6)]
+        couple.append(jnp.concatenate(blocks, axis=0).astype(BF))
+    couple = jnp.concatenate(couple, axis=1)
+    gsend_ref[0] = dot(couple, x_ref[0:ROWS, E - HALO : E]).astype(BF)
+    gsend_ref[1] = dot(couple, x_ref[0:ROWS, 0:HALO]).astype(BF)
+
     pl.semaphore_wait(barrier, len(greeted))
+    first = [
+        copy(gsend_ref.at[0], grecv_ref.at[0], g_s.at[0], g_r.at[0], right),
+        copy(gsend_ref.at[1], grecv_ref.at[1], g_s.at[1], g_r.at[1], left),
+    ]
+    for c in first:
+        c.start()
     rim0 = rims(0)
     for c in rim0:
         c.start()
@@ -169,63 +208,22 @@
         copy(x_ref.at[0:ROWS, E - HALO : E], hlo_ref, flow_s.at[0], flow_r.at[0], right),
         copy(x_ref.at[0:ROWS, 0:HALO], hhi_ref, flow_s.at[1], flow_r.at[1], left),
     ]
+
     for c in flow:
         c.start()
 
-    for c in fetch[1:]:
-        c.wait()
-    penalty = None
-    for v in range(VARS):
-        total = jnp.max(jnp.sum(jnp.abs(flux_ref[v]), axis=1, keepdims=True), axis=0, keepdims=True)
-        penalty = total if penalty is None else jnp.maximum(penalty, total)
-
-    def flux(d, v, w):
-        return flux_ref[v, d : d + 1, w : w + 1]
-
-    for v in range(VARS):
+    def spread_faces(values, part):
+        for face in range(6):
+            g_ref[face, part * 32 : part * 32 + 32, :] = values[face * 32 : face * 32 + 32]
+
+    def operator(v):
         for w in range(VARS):
             block = flux(0, v, w) * own_ref[0] + flux(1, v, w) * own_ref[1] + flux(2, v, w) * own_ref[2]
             if v == w:
                 block = block + penalty * own_ref[3]
             ab_ref[v * 128 : v * 128 + 128, w * 128 : w * 128 + 128] = block.astype(BF)
-    column = iota((1, 128), 1)
-    for face in range(6):
-        sign = 1.0 if face % 2 else -1.0
-        where = place_ref[face].astype(F32)
-        for v in range(VARS):
-            factor = jnp.zeros((1, 128), F32)
-            for w in range(VARS):
-                value = sign * flux(face // 2, v, w)
-                if v == w:
-                    value = value - penalty
-                factor = jnp.where((column >= 25 * w) & (column < 25 * w + 25), value, factor)
-            ab_ref[v * 128 : v * 128 + 128, ROWS + face * 128 : ROWS + face * 128 + 128] = (where * factor).astype(BF)
-
-    def extract(values, part, lanes):
-        e = [dot(select_ref[w], values(w)) for w in range(VARS)]
-        for face in range(6):
-            g = [x[face * 32 : face * 32 + 32] for x in e]
-            pieces = [g[0][0:24]]
-            for w in range(1, VARS):
-                pieces += [g[w - 1][24:32] + g[w][0:8], g[w][8:24]]
-            pieces += [g[VARS - 1][24:32]]
-            src_ref[face, pl.ds(part * 128, 128), lanes] = jnp.concatenate(pieces, axis=0).astype(BF)
-
-    for part in range(E // PART):
-        for half in range(PART // TILE):
-            cols = slice(part * PART + half * TILE, part * PART + (half + 1) * TILE)
-            extract(lambda w: x_ref[w * 128 : w * 128 + 128, cols], part, slice(half * TILE, (half + 1) * TILE))
-
-    relative = (owner_ref[...] - dom + N_DOM) & (N_DOM - 1)
-    owned = one_hot(relative, N_DOM)
-    earlier = (iota((F, F), 0) < iota((F, F), 1)).astype(F32).astype(BF)
-    rank = jnp.sum(owned * dot(owned.astype(BF), earlier), axis=0, keepdims=True).astype(I32)
-    ohs_ref[...] = one_hot(rank, CAP).astype(BF)
-
-    payload = jnp.concatenate([weight_ref[...], patch_ref[...].astype(F32), jnp.zeros((15, F), F32)], axis=0)
-    payload = jnp.concatenate([payload * owned[d : d + 1] for d in range(N_DOM)], axis=0)
-    placed = dot_t(payload.astype(BF), ohs_ref[...])
-    wsend_ref[...] = placed.astype(BF).reshape(N_DOM, 32, CAP)
+
+    operator(VARS - 1)
 
     last = slice((VARS - 1) * 128, VARS * 128)
     elems = selem_ref[...]
@@ -233,7 +231,8 @@
     base, near = jnp.zeros((128, F), F32), jnp.zeros((16, F), F32)
     for h in range(E // TILE):
         cols = slice(h * TILE, (h + 1) * TILE)
-        factor = FLOW_STEP * jac_ref[:, cols]
+        factor = _STEP * jac_ref[:, cols]
+        spread_faces(dot(couple, x_ref[0:ROWS, cols]).astype(BF), h + 1)
         moved = x_ref[last, cols].astype(F32) + factor * dot(ab_ref[last, 0:ROWS], x_ref[0:ROWS, cols])
         ids = nb_ref[:, cols]
         rows = jnp.concatenate(
@@ -245,20 +244,101 @@
         base = jnp.where(mine, joined(found[0:256]), base)
         near = jnp.where(mine, found[256:272], near)
     surf_factor = near[0:1] + near[1:2]
-    surf_near = near[2:8].astype(I32) + 256 * near[8:14].astype(I32)
+    column_of, block_of = near[2:8].astype(I32), near[8:14].astype(I32)
+
+    payload = jnp.concatenate([weight_ref[...], patch_ref[...].astype(F32), jnp.zeros((15, F), F32)], axis=0)
+    payload = jnp.concatenate([payload * owned[d : d + 1] for d in range(N_DOM)], axis=0)
+    placed = dot_t(payload.astype(BF), ohs_ref[...])
+    wsend_ref[...] = placed.astype(BF).reshape(N_DOM, 32, CAP)
+
+    early = [copy(wsend_ref.at[d], wrecv_ref.at[d], w_s.at[0], w_r.at[0], dom_peer(d)) for d in range(1, N_DOM)]
+    for c in early:
+        c.start()
+    wrecv_ref[0] = wsend_ref[0]
 
     for k in range(K):
         ids = pnode_ref[k : k + 1, :]
         lanes = slice(k * PATCHES, (k + 1) * PATCHES)
         ohn_ref[:, lanes] = one_hot(ids & 127, 128).astype(BF)
         maskn_ref[:, lanes] = one_hot(ids >> 7, 8)
-    for q in range(4):
-        ids = conn_ref[q : q + 1, :]
-        ids = jnp.where(ids >= HS, ids - HS, ids + (S + 128 - HS))
-        lanes = slice(q * SE, (q + 1) * SE)
-        ohc_ref[:, lanes] = one_hot(ids & 127, 128).astype(BF)
-        maskc_ref[:, lanes] = one_hot(ids >> 7, 8)
-        mask8_ref[:, lanes] = ((ids >> 7) == 8).astype(F32)
+    for v in range(VARS - 1):
+        operator(v)
+    column = iota((1, 128), 1)
+    for face in range(6):
+        where = place_ref[face].astype(F32)
+        for v in range(VARS):
+            factor = jnp.zeros((1, 128), F32)
+            for w in range(VARS):
+                factor = jnp.where((column >= 25 * w) & (column < 25 * w + 25), coupling(face, v, w), factor)
+            ab_ref[v * 128 : v * 128 + 128, ROWS + face * 128 : ROWS + face * 128 + 128] = (where * factor).astype(BF)
+
+    for c in first:
+        c.wait()
+    keep_hi = jnp.where(line < devices - 1, 1.0, 0.0).astype(BF)
+    keep_lo = jnp.where(line > 0, 1.0, 0.0).astype(BF)
+    spread_faces(grecv_ref[0] * keep_lo, 0)
+    spread_faces(grecv_ref[1] * keep_hi, E // HALO + 1)
+    n = iota((32, F), 0)
+    i, j = (n * 13) >> 6, n - 5 * ((n * 13) >> 6)
+    added = jnp.zeros((32, F), F32)
+    for face in range(6):
+        picked = dot(g_ref[face], one_hot(column_of[face : face + 1], HALO).astype(BF))
+        block = block_of[face : face + 1]
+        other = picked[0:32]
+        for p in range(1, E // HALO + 2):
+            other = jnp.where(block == p, picked[p * 32 : p * 32 + 32], other)
+        node = (n, n + 100, 25 * i + j, 25 * i + j + 20, 5 * n, 5 * n + 4)[face]
+        added = added + jnp.where((node == snode_ref[...]) & (n < 25), other, 0.0)
+    own_part = jnp.sum(jnp.where(iota((128, F), 0) == snode_ref[...], base, 0.0), axis=0, keepdims=True)
+    pressure = own_part + surf_factor * jnp.sum(added, axis=0, keepdims=True)
+    pressure = pressure.astype(BF).astype(F32)
+    traction = jnp.concatenate([normal_ref[...] * pressure, jnp.zeros((5, F), F32)], axis=0)
+    rows = jnp.concatenate([traction * owned[d : d + 1] for d in range(N_DOM)], axis=0)
+    tsend_ref[...] = joined(dot_t(halves(rows), ohs_ref[...])).reshape(N_DOM, 8, CAP)
+    loads = [copy(tsend_ref.at[d], trecv_ref.at[d], t_s.at[0], t_r.at[0], dom_peer(d)) for d in range(1, N_DOM)]
+    for c in loads:
+        c.start()
+    trecv_ref[0] = tsend_ref[0]
+
+    def neighbour(face, ids):
+        ids = jnp.where(ids >= HALO, ids - HALO, ids + (E + HALO))
+        picked = dot(src_ref[face], one_hot(ids & (PART - 1), PART).astype(BF))
+        part = ids // PART
+        other = picked[0:128]
+        for p in range(1, PARTS):
+            other = jnp.where(part == p, picked[p * 128 : p * 128 + 128], other)
+        return other.astype(BF)
+
+    def advance(t, carry):
+        cols = pl.ds(pl.multiple_of(t * TILE, TILE), TILE)
+        for face in range(6):
+            x_ref[ROWS + face * 128 : ROWS + face * 128 + 128, cols] = neighbour(face, nb_ref[face : face + 1, cols])
+        factor = _STEP * jac_ref[:, cols]
+        change = dot(ab_ref[...], x_ref[:, cols])
+        for v in range(VARS):
+            moved = x_ref[v * 128 : v * 128 + 128, cols].astype(F32) + factor * change[v * 128 : v * 128 + 128]
+            fluid_ref[v, :, cols] = moved.astype(BF)[:NP]
+        return carry
+
+    tiles = (0, 3, 2, 3)
+
+    def fill(wait):
+        lax.fori_loop(sum(tiles[:wait]), sum(tiles[: wait + 1]), advance, 0, unroll=True)
+
+    def extract(values, part, lanes):
+        e = [dot(select_ref[w], values(w)) for w in range(VARS)]
+        for face in range(6):
+            g = [x[face * 32 : face * 32 + 32] for x in e]
+            pieces = [g[0][0:24]]
+            for w in range(1, VARS):
+                pieces += [g[w - 1][24:32] + g[w][0:8], g[w][8:24]]
+            pieces += [g[VARS - 1][24:32]]
+            src_ref[face, pl.ds(part * 128, 128), lanes] = jnp.concatenate(pieces, axis=0).astype(BF)
+
+    for part in range(E // PART):
+        for half in range(PART // TILE):
+            cols = slice(part * PART + half * TILE, part * PART + (half + 1) * TILE)
+            extract(lambda w: x_ref[w * 128 : w * 128 + 128, cols], part, slice(half * TILE, (half + 1) * TILE))
 
     def internal(step):
         lane = iota((8, 128), 1)
@@ -281,71 +361,26 @@
             spread.append(line_c * maskc_ref[...])
         return joined(dot_t(halves(jnp.concatenate(spread, axis=0)), ohc_ref[...]))
 
+    for q in range(4):
+        ids = conn_ref[q : q + 1, :]
+        ids = jnp.where(ids >= HS, ids - HS, ids + (S + 128 - HS))
+        lanes = slice(q * SE, (q + 1) * SE)
+        ohc_ref[:, lanes] = one_hot(ids & 127, 128).astype(BF)
+        maskc_ref[:, lanes] = one_hot(ids >> 7, 8)
+        mask8_ref[:, lanes] = ((ids >> 7) == 8).astype(F32)
+
     for c in rim0:
         c.wait()
     inner = internal(0)
 
-    for c in flow:
-        c.wait()
-    early = [copy(wsend_ref.at[d], wrecv_ref.at[d], w_s.at[d], w_r.at[d], dom_peer(d)) for d in range(1, N_DOM)]
-    for c in early:
-        c.start()
-    wrecv_ref[0] = wsend_ref[0]
-    keep_hi = jnp.where(line < devices - 1, 1.0, 0.0).astype(BF)
-    keep_lo = jnp.where(line > 0, 1.0, 0.0).astype(BF)
-    extract(lambda w: hhi_ref[w * 128 : w * 128 + 128, :] * keep_hi, PARTS - 1, slice(0, HALO))
-    extract(lambda w: hlo_ref[w * 128 : w * 128 + 128, :] * keep_lo, PARTS - 1, slice(HALO, 2 * HALO))
-
-    def neighbour(face, ids):
-        ids = jnp.where(ids >= HALO, ids - HALO, ids + (E + HALO))
-        picked = dot(src_ref[face], one_hot(ids & (PART - 1), PART).astype(BF))
-        part = ids // PART
-        other = picked[0:128]
-        for p in range(1, PARTS):
-            other = jnp.where(part == p, picked[p * 128 : p * 128 + 128], other)
-        return other.astype(BF)
-
-    for half in range(F // TILE):
-        cols = slice(half * TILE, (half + 1) * TILE)
-        for face in range(6):
-            surf_ref[face * 128 : face * 128 + 128, cols] = neighbour(face, surf_near[face : face + 1, cols])
-    found = base + surf_factor * dot(ab_ref[last, ROWS:DEPTH], surf_ref[...])
-    found = found.astype(BF).astype(F32)
-    pressure = jnp.sum(jnp.where(iota((128, F), 0) == snode_ref[...], found, 0.0), axis=0, keepdims=True)
-    traction = jnp.concatenate([normal_ref[...] * pressure, jnp.zeros((5, F), F32)], axis=0)
-    rows = jnp.concatenate([traction * owned[d : d + 1] for d in range(N_DOM)], axis=0)
-    tsend_ref[...] = joined(dot_t(halves(rows), ohs_ref[...])).reshape(N_DOM, 8, CAP)
-    loads = [copy(tsend_ref.at[d], trecv_ref.at[d], t_s.at[d], t_r.at[d], dom_peer(d)) for d in range(1, N_DOM)]
-    for c in loads:
-        c.start()
-    trecv_ref[0] = tsend_ref[0]
-
-    def advance(t, carry):
-        cols = pl.ds(pl.multiple_of(t * TILE, TILE), TILE)
-        for face in range(6):
-            x_ref[ROWS + face * 128 : ROWS + face * 128 + 128, cols] = neighbour(face, nb_ref[face : face + 1, cols])
-        factor = FLOW_STEP * jac_ref[:, cols]
-        change = dot(ab_ref[...], x_ref[:, cols])
-        for v in range(VARS):
-            moved = x_ref[v * 128 : v * 128 + 128, cols].astype(F32) + factor * change[v * 128 : v * 128 + 128]
-            fluid_ref[v, :, cols] = moved.astype(BF)[:NP]
-        return carry
-
-    tiles = (2, 2, 2, 2)
-
-    def fill(wait):
-        lax.fori_loop(sum(tiles[:wait]), sum(tiles[: wait + 1]), advance, 0)
-
-    for c in early:
-        c.wait()
+    all_of(wsend_ref, wrecv_ref, w_s, w_r).wait()
     for d in range(N_DOM):
         block = wrecv_ref[d].astype(F32)
         wall_ref[:, d * CAP : (d + 1) * CAP] = block[0:K]
         ohp_ref[:, d * CAP : (d + 1) * CAP] = one_hot(block[K : K + 1].astype(I32), PATCHES).astype(BF)
     fill(0)
 
-    for c in loads:
-        c.wait()
+    all_of(tsend_ref, trecv_ref, t_s, t_r).wait()
     load = []
     for c in range(3):
         line_c = jnp.concatenate([trecv_ref[d, c : c + 1, :] for d in range(N_DOM)], axis=1)
@@ -357,13 +392,17 @@
         spread.append(line_c * maskn_ref[...])
     partial = joined(dot_t(halves(jnp.concatenate(spread, axis=0)), ohn_ref[...]))
     ebuf_ref[...] = partial
-    sums = [copy(ebuf_ref, erecv_ref.at[d], e_s.at[d], e_r.at[d], sec_peer(d)) for d in range(1, N_SEC)]
+    sums = [copy(ebuf_ref, erecv_ref.at[d], e_s.at[0], e_r.at[0], sec_peer(d)) for d in range(1, N_SEC)]
     for c in sums:
         c.start()
     erecv_ref[0] = partial
+
+    for c in flow:
+        c.wait()
+    extract(lambda w: hhi_ref[w * 128 : w * 128 + 128, :] * keep_hi, PARTS - 1, slice(0, HALO))
+    extract(lambda w: hlo_ref[w * 128 : w * 128 + 128, :] * keep_lo, PARTS - 1, slice(HALO, 2 * HALO))
     fill(1)
-    for c in sums:
-        c.wait()
+    all_of(erecv_ref, erecv_ref, e_s, e_r).wait()
     external = erecv_ref[lax.rem(sec, N_SEC)]
     for s in range(1, N_SEC):
         external = external + erecv_ref[lax.rem(sec - s + N_SEC, N_SEC)]
@@ -395,7 +434,7 @@
         for d in range(N_DOM):
             rsend_ref[d, c : c + 1, :] = total[:, d * CAP : (d + 1) * CAP]
     returns = [
-        copy(rsend_ref.at[d], rrecv_ref.at[d], r_s.at[d], r_r.at[d], dom_peer(N_DOM - d)) for d in range(1, N_DOM)
+        copy(rsend_ref.at[d], rrecv_ref.at[d], r_s.at[0], r_r.at[0], dom_peer(N_DOM - d)) for d in range(1, N_DOM)
     ]
     for c in returns:
         c.start()
@@ -404,8 +443,7 @@
         for c in range(3):
             shell_ref[c : c + 1, h * 128 : (h + 1) * 128] = d_ref[c * 8 + h : c * 8 + h + 1, :]
     fill(3)
-    for c in returns:
-        c.wait()
+    all_of(rsend_ref, rrecv_ref, r_s, r_r).wait()
     back = joined(dot(halves(rrecv_ref[...].reshape(N_DOM * 8, CAP)), ohs_ref[...]))
     shift = back[0:8] * owned[0:1]
     for d in range(1, N_DOM):
@@ -439,7 +477,9 @@
             pltpu.VMEM((ROWS, DEPTH), BF),
             pltpu.VMEM((ROWS, HALO), BF),
             pltpu.VMEM((ROWS, HALO), BF),
-            pltpu.VMEM((6 * 128, F), BF),
+            pltpu.VMEM((6, (E // HALO + 2) * 32, HALO), BF),
+            pltpu.VMEM((2, 6 * 32, HALO), BF),
+            pltpu.VMEM((2, 6 * 32, HALO), BF),
             pltpu.VMEM((PATCHES, N_DOM * CAP), BF),
             pltpu.VMEM((128, K * PATCHES), BF),
             pltpu.VMEM((8, K * PATCHES), F32),
@@ -461,11 +501,11 @@
             pltpu.VMEM((24, 128), F32),
             pltpu.VMEM((24, 128), F32),
             pltpu.VMEM((8, 128), F32),
-            dma((4,)), dma((2,)), dma((2,)),
-            dma((N_DOM,)), dma((N_DOM,)),
-            dma((N_DOM,)), dma((N_DOM,)),
-            dma((N_DOM,)), dma((N_DOM,)),
-            dma((N_SEC,)), dma((N_SEC,)),
+            dma((4,)), dma((2,)), dma((2,)), dma((2,)), dma((2,)),
+            dma((1,)), dma((1,)),
+            dma((1,)), dma((1,)),
+            dma((1,)), dma((1,)),
+            dma((1,)), dma((1,)),
             dma((STEPS, 2)), dma((STEPS, 2)),
         ],
         compiler_params=pltpu.CompilerParams(

time: 49.5 us -> 46.8 us (0.945)
  the two profiles are of different devices: /device:TPU:0 before, /device:TPU:1 now
where the time goes in v3:
time: 46.8 us; the launch traced here: 46.6 us
  Pallas kernels  43.2 us (92%)
  local copies, waits for them, and re-layouts  2.7 us (6%)
  between operations  0.65 us (1%)
    pallas_call x1, Pallas kernels, on_device(): pl.pallas_call(kernel, out_shape=(pltpu.VMEM((VARS, NP, E), BF), pltpu.VM...  43.2 us
    unnamed x3, local copies, waits for them, and re-layouts  2.7 us

profile of v3, /device:TPU:1, one launch (start us, length us, event | category | flops | bytes accessed | tf_op | source)
XLA Modules:
  0.0 46.6 jit_solution(6733287707262428487)
XLA Ops:
  0.6 43.2 %shard_map.211 = (bf16[5,125,2048]{2,1,0:T(8,128)(2,1)S(1)}, f32[3,1024]{1,0:T(4,128)S(1)}, f32[3,512]{1,0:T(4,128)S(1)}) custom-call(bf16[5,125,2048]{2,1,0:T(8,128)(2,1)} %state_ref.1, f32[1,2048]{1,0:T(1,128)} %bitcast.9, f32[5,3,5]{2,1,0:T(4,128)} %bitcast.8, s32[6,2048]{1,0:T(8,128)} %nb_ref.1, s32[1,512]{1,0:T(1,128)} %bitcast.12, s32[1,512]{1,0:T(1,128)} %bitcast.13, ...), custom_call_target="tpu_custom_call" | custom-call | tf_op jit(solution)/shard_map/pallas_call | solution.py:461
  43.9 1.5 %copy.26 = bf16[5,125,2048]{2,1,0:T(8,128)(2,1)} copy(bf16[5,125,2048]{2,1,0:T(8,128)(2,1)S(1)} %get-tuple-element.3) | data formatting | bytes 5120000
  45.4 0.6 %copy.28 = f32[3,512]{1,0:T(4,128)} copy(f32[3,512]{1,0:T(4,128)S(1)} %get-tuple-element.5) | data formatting | bytes 12288
  46.0 0.6 %copy.27 = f32[3,1024]{1,0:T(4,128)} copy(f32[3,1024]{1,0:T(4,128)S(1)} %get-tuple-element.4) | data formatting | bytes 24576

commit v4 on v3

--- a/solution.py
+++ b/solution.py
@@ -16,6 +16,7 @@
 PART = 512
 PARTS = (E + 2 * HALO) // PART
 ROWS = VARS * 128
+SPLIT = 3 * 128
 DEPTH = ROWS + 6 * 128
 BF, F32, I32 = jnp.bfloat16, jnp.float32, jnp.int32
 HIGHEST = lax.Precision.HIGHEST
@@ -205,11 +206,13 @@
     for c in rim0:
         c.start()
     flow = [
-        copy(x_ref.at[0:ROWS, E - HALO : E], hlo_ref, flow_s.at[0], flow_r.at[0], right),
-        copy(x_ref.at[0:ROWS, 0:HALO], hhi_ref, flow_s.at[1], flow_r.at[1], left),
+        (
+            copy(x_ref.at[rows, E - HALO : E], hlo_ref.at[rows], flow_s.at[0, lot], flow_r.at[0, lot], right),
+            copy(x_ref.at[rows, 0:HALO], hhi_ref.at[rows], flow_s.at[1, lot], flow_r.at[1, lot], left),
+        )
+        for lot, rows in enumerate((slice(0, SPLIT), slice(SPLIT, ROWS)))
     ]
-
-    for c in flow:
+    for c in flow[0]:
         c.start()
 
     def spread_faces(values, part):
@@ -298,6 +301,8 @@
     loads = [copy(tsend_ref.at[d], trecv_ref.at[d], t_s.at[0], t_r.at[0], dom_peer(d)) for d in range(1, N_DOM)]
     for c in loads:
         c.start()
+    for c in flow[1]:
+        c.start()
     trecv_ref[0] = tsend_ref[0]
 
     def neighbour(face, ids):
@@ -397,8 +402,9 @@
         c.start()
     erecv_ref[0] = partial
 
-    for c in flow:
-        c.wait()
+    for lot in flow:
+        for c in lot:
+            c.wait()
     extract(lambda w: hhi_ref[w * 128 : w * 128 + 128, :] * keep_hi, PARTS - 1, slice(0, HALO))
     extract(lambda w: hlo_ref[w * 128 : w * 128 + 128, :] * keep_lo, PARTS - 1, slice(HALO, 2 * HALO))
     fill(1)
@@ -501,7 +507,7 @@
             pltpu.VMEM((24, 128), F32),
             pltpu.VMEM((24, 128), F32),
             pltpu.VMEM((8, 128), F32),
-            dma((4,)), dma((2,)), dma((2,)), dma((2,)), dma((2,)),
+            dma((4,)), dma((2,)), dma((2,)), dma((2, 2)), dma((2, 2)),
             dma((1,)), dma((1,)),
             dma((1,)), dma((1,)),
             dma((1,)), dma((1,)),

time: 46.8 us -> 46 us (0.983)
  the two profiles are of different devices: /device:TPU:1 before, /device:TPU:0 now
where the time goes in v4:
time: 46 us; the launch traced here: 45.8 us
  Pallas kernels  42.5 us (92%)
  local copies, waits for them, and re-layouts  2.7 us (6%)
  between operations  0.65 us (1%)
    pallas_call x1, Pallas kernels, on_device(): pl.pallas_call(kernel, out_shape=(pltpu.VMEM((VARS, NP, E), BF), pltpu.VM...  42.5 us
    unnamed x3, local copies, waits for them, and re-layouts  2.7 us

profile of v4, /device:TPU:0, one launch (start us, length us, event | category | flops | bytes accessed | tf_op | source)
XLA Modules:
  0.0 45.8 jit_solution(2618508234014483950)
XLA Ops:
  0.6 42.5 %shard_map.211 = (bf16[5,125,2048]{2,1,0:T(8,128)(2,1)S(1)}, f32[3,1024]{1,0:T(4,128)S(1)}, f32[3,512]{1,0:T(4,128)S(1)}) custom-call(bf16[5,125,2048]{2,1,0:T(8,128)(2,1)} %state_ref.1, f32[1,2048]{1,0:T(1,128)} %bitcast.9, f32[5,3,5]{2,1,0:T(4,128)} %bitcast.8, s32[6,2048]{1,0:T(8,128)} %nb_ref.1, s32[1,512]{1,0:T(1,128)} %bitcast.12, s32[1,512]{1,0:T(1,128)} %bitcast.13, ...), custom_call_target="tpu_custom_call" | custom-call | tf_op jit(solution)/shard_map/pallas_call | solution.py:467
  43.1 1.5 %copy.26 = bf16[5,125,2048]{2,1,0:T(8,128)(2,1)} copy(bf16[5,125,2048]{2,1,0:T(8,128)(2,1)S(1)} %get-tuple-element.3) | data formatting | bytes 5120000
  44.6 0.6 %copy.28 = f32[3,512]{1,0:T(4,128)} copy(f32[3,512]{1,0:T(4,128)S(1)} %get-tuple-element.5) | data formatting | bytes 12288
  45.2 0.6 %copy.27 = f32[3,1024]{1,0:T(4,128)} copy(f32[3,1024]{1,0:T(4,128)S(1)} %get-tuple-element.4) | data formatting | bytes 24576

commit v5 on v4

--- a/solution.py
+++ b/solution.py
@@ -16,7 +16,7 @@
 PART = 512
 PARTS = (E + 2 * HALO) // PART
 ROWS = VARS * 128
-SPLIT = 3 * 128
+SPLIT = 4 * 128
 DEPTH = ROWS + 6 * 128
 BF, F32, I32 = jnp.bfloat16, jnp.float32, jnp.int32
 HIGHEST = lax.Precision.HIGHEST

time: 46 us -> 46 us (level)
  no operation moved by 1% of the time
where the time goes in v5:
time: 46 us; the launch traced here: 45.9 us
  Pallas kernels  42.5 us (92%)
  local copies, waits for them, and re-layouts  2.7 us (6%)
  between operations  0.65 us (1%)
    pallas_call x1, Pallas kernels, on_device(): pl.pallas_call(kernel, out_shape=(pltpu.VMEM((VARS, NP, E), BF), pltpu.VM...  42.5 us
    unnamed x3, local copies, waits for them, and re-layouts  2.7 us

profile of v5, /device:TPU:0, one launch (start us, length us, event | category | flops | bytes accessed | tf_op | source)
XLA Modules:
  0.0 45.9 jit_solution(8068852824757386002)
XLA Ops:
  0.6 42.5 %shard_map.211 = (bf16[5,125,2048]{2,1,0:T(8,128)(2,1)S(1)}, f32[3,1024]{1,0:T(4,128)S(1)}, f32[3,512]{1,0:T(4,128)S(1)}) custom-call(bf16[5,125,2048]{2,1,0:T(8,128)(2,1)} %state_ref.1, f32[1,2048]{1,0:T(1,128)} %bitcast.9, f32[5,3,5]{2,1,0:T(4,128)} %bitcast.8, s32[6,2048]{1,0:T(8,128)} %nb_ref.1, s32[1,512]{1,0:T(1,128)} %bitcast.12, s32[1,512]{1,0:T(1,128)} %bitcast.13, ...), custom_call_target="tpu_custom_call" | custom-call | tf_op jit(solution)/shard_map/pallas_call | solution.py:467
  43.2 1.5 %copy.26 = bf16[5,125,2048]{2,1,0:T(8,128)(2,1)} copy(bf16[5,125,2048]{2,1,0:T(8,128)(2,1)S(1)} %get-tuple-element.3) | data formatting | bytes 5120000
  44.7 0.6 %copy.28 = f32[3,512]{1,0:T(4,128)} copy(f32[3,512]{1,0:T(4,128)S(1)} %get-tuple-element.5) | data formatting | bytes 12288
  45.3 0.6 %copy.27 = f32[3,1024]{1,0:T(4,128)} copy(f32[3,1024]{1,0:T(4,128)S(1)} %get-tuple-element.4) | data formatting | bytes 24576
